TPU v7x, 32 devices: a whole 2x2x4 slice. The times are simulated.
32 devices in a mesh: fsdp: 16 (over z, y, x), tp: 2 (over core).
Axes of the slice: x: 2, y: 2, z: 4, core: 2. Of those that a mesh axis runs over, the one named last changes fastest.
Arguments:
- tokens: bfloat16 [8192, 768], P(('fsdp', 'tp')), may hold values from -6 to 6
- cotangent: bfloat16 [8192, 768], P(('fsdp', 'tp')), may hold values from -6 to 6
- gain_attn: bfloat16 [768], replicated, may hold values from 0.25 to 1.75
- gain_moe: bfloat16 [768], replicated, may hold values from 0.25 to 1.75
- w_query: bfloat16 [768, 768], P('fsdp', 'tp'), may hold values from -0.21875 to 0.21875
- w_key: bfloat16 [768, 768], P('fsdp', 'tp'), may hold values from -0.21875 to 0.21875
- w_value: bfloat16 [768, 768], P('fsdp', 'tp'), may hold values from -0.21875 to 0.21875
- w_output: bfloat16 [768, 768], P('tp', 'fsdp'), may hold values from -0.875 to 0.875
- bias_table: bfloat16 [32, 12], P(None, 'tp'), may hold values from -4 to 4
- router: bfloat16 [768, 4], replicated, may hold values from -0.15625 to 0.15625
- w_in: bfloat16 [4, 768, 3072], P(None, 'fsdp', 'tp'), may hold values from -0.21875 to 0.21875
- w_out: bfloat16 [4, 3072, 768], P(None, 'tp', 'fsdp'), may hold values from -0.4375 to 0.4375
- lengths: int32 [16, 4], P('fsdp'), may hold values from 1 to 256, as said below
- routes: int32 [8192], P('fsdp'), may hold values from 0 to 3
- slots: int32 [8192], P('fsdp'), may hold values from -1 to 191, as said below
- buckets: int32 [511], replicated, may hold values from 0 to 31
Outputs:
- output: bfloat16 [8192, 768], P(('fsdp', 'tp'))
- grad_tokens: float32 [8192, 768], P(('fsdp', 'tp'))
- grad_gain_attn: float32 [768], replicated
- grad_gain_moe: float32 [768], replicated
- grad_w_query: float32 [768, 768], P('fsdp', 'tp')
- grad_w_key: float32 [768, 768], P('fsdp', 'tp')
- grad_w_value: float32 [768, 768], P('fsdp', 'tp')
- grad_w_output: float32 [768, 768], P('tp', 'fsdp')
- grad_bias_table: float32 [32, 12], P(None, 'tp')
- grad_router: float32 [768, 4], replicated
- grad_w_in: float32 [4, 768, 3072], P(None, 'fsdp', 'tp')
- grad_w_out: float32 [4, 3072, 768], P(None, 'tp', 'fsdp')
Inputs may be any that keep to these rules, and one draw needn't show every extreme that they name: Each group holds 4 sequences whose lengths sum to 512; the second is the longest, of exactly 256 tokens. A token's slot is the number of earlier tokens of its group with the same route, or -1 where that number is 192 or more; in every group some expert fills all 192 slots.
All inputs are finite; a program needn't handle non-finite values.
Results may differ from a plain program's by a relative error of at most 0.013.
Values may be sent and summed in bfloat16 or wider, within the bound.
A program may use at most 256 MiB of HBM per device.

v0:
```python
import math

import jax
import jax.numpy as jnp
from jax import lax
from jax.sharding import PartitionSpec as P

HD = 64
CAP = 192


EPSILON = 1e-06
MASKED = -1e30
HIGHEST = lax.Precision.HIGHEST


def rms_stats(values):
    inverse = lax.rsqrt(jnp.mean(values * values, axis=-1, keepdims=True) + EPSILON)
    return (values * inverse, inverse)


def rms_back(grad_hat, normed, inverse):
    return inverse * (grad_hat - normed * jnp.mean(grad_hat * normed, axis=-1, keepdims=True))


def diagonal_sums(grid):
    head_count, block_rows, key_count = grid.shape
    line_len = key_count + block_rows
    padded = jnp.pad(grid[:, ::-1, :], ((0, 0), (0, 0), (0, block_rows)))
    skewed = padded.reshape(head_count, block_rows * line_len)[:, : block_rows * (line_len - 1)]
    return jnp.sum(skewed.reshape(head_count, block_rows, line_len - 1), axis=1)


def toeplitz_block(window, block_rows, key_count):
    head_count, window_len = window.shape
    tiled = jnp.tile(window, (1, block_rows + 1))[:, : block_rows * (window_len + 1)]
    skewed = tiled.reshape(head_count, block_rows, window_len + 1)[:, :, :key_count]
    return skewed[:, ::-1, :]


def on_device(
    tokens,
    cotangent,
    gain_attn,
    gain_moe,
    w_query,
    w_key,
    w_value,
    w_output,
    bias_table,
    router,
    w_in,
    w_out,
    lengths,
    routes,
    slots,
    buckets,
):
    row_count, model_width = tokens.shape
    group_rows = routes.shape[0]
    bucket_count, head_count = bias_table.shape
    expert_count = router.shape[1]
    slot_count = expert_count * CAP
    block_rows = min(512, group_rows)
    block_count = group_rows // block_rows
    span_len = buckets.shape[0]
    max_len = (span_len + 1) // 2
    score_scale = 1.0 / math.sqrt(HD)
    tp_index = lax.axis_index("tp")
    positions = jnp.arange(group_rows, dtype=jnp.int32)
    expert_ids = jnp.arange(expert_count, dtype=jnp.int32)
    inputs = tokens.astype(jnp.float32)
    gain_one = gain_attn.astype(jnp.float32)
    gain_two = gain_moe.astype(jnp.float32)
    normed_one, inverse_one = rms_stats(inputs)
    scaled_one = (normed_one * gain_one).astype(jnp.bfloat16)
    rows_one = lax.all_gather(scaled_one, "tp", axis=0, tiled=True)
    query_full, key_full, value_full, output_full = (
        lax.all_gather(w_query, "fsdp", axis=0, tiled=True),
        lax.all_gather(w_key, "fsdp", axis=0, tiled=True),
        lax.all_gather(w_value, "fsdp", axis=0, tiled=True),
        lax.all_gather(w_output, "fsdp", axis=1, tiled=True),
    )
    queries = jnp.dot(rows_one, query_full, preferred_element_type=jnp.float32).astype(jnp.bfloat16)
    keys_all = jnp.dot(rows_one, key_full, preferred_element_type=jnp.float32).astype(jnp.bfloat16)
    values_all = jnp.dot(rows_one, value_full, preferred_element_type=jnp.float32).astype(
        jnp.bfloat16
    )
    query_heads = queries.reshape(group_rows, head_count, HD)
    key_heads = keys_all.reshape(group_rows, head_count, HD)
    value_heads = values_all.reshape(group_rows, head_count, HD)
    bounds = jnp.cumsum(lengths[0])
    segment = jnp.sum((positions[:, None] >= bounds[None, :]).astype(jnp.int32), axis=1)
    bucket_ids = jnp.arange(bucket_count, dtype=jnp.int32)
    bucket_hot = (buckets[:, None] == bucket_ids[None, :]).astype(jnp.float32)
    wide_offsets = jnp.clip(
        jnp.arange(2 * group_rows - 1, dtype=jnp.int32) - group_rows + max_len, 0, span_len - 1
    )
    wide_hot = (jnp.take(buckets, wide_offsets, axis=0)[:, None] == bucket_ids[None, :]).astype(
        jnp.float32
    )
    extended = jnp.dot(wide_hot, bias_table.astype(jnp.float32), precision=HIGHEST).T

    def block_scores():
        bias_blk = toeplitz_block(extended, block_rows, group_rows)
        raw_scores = (
            jnp.einsum("qhd,khd->hqk", query_heads, key_heads, preferred_element_type=jnp.float32)
            * score_scale
            + bias_blk
        )
        same_seq = segment[:, None] == segment[None, :]
        return (jnp.where(same_seq[None], raw_scores, MASKED), query_heads)

    def attend(first_row):
        scores, query_blk = block_scores()
        top_score = jnp.max(scores, axis=-1, keepdims=True)
        raised = jnp.exp(scores - top_score)
        row_total = jnp.sum(raised, axis=-1, keepdims=True)
        weights_p = (raised / row_total).astype(jnp.bfloat16)
        mixed_blk = jnp.einsum(
            "hqk,khd->qhd", weights_p, value_heads, preferred_element_type=jnp.float32
        )
        return (mixed_blk, (top_score + jnp.log(row_total))[..., 0])

    block_starts = jnp.arange(block_count, dtype=jnp.int32) * block_rows
    mixed_blocks, log_totals = lax.map(attend, block_starts)
    mixed_out = mixed_blocks.reshape(group_rows, head_count * HD).astype(jnp.bfloat16)
    attn_part = jnp.dot(mixed_out, output_full, preferred_element_type=jnp.float32)
    attn_rows = lax.psum_scatter(attn_part, "tp", scatter_dimension=0, tiled=True)
    hidden = inputs + attn_rows
    normed_two, inverse_two = rms_stats(hidden)
    scaled_two = (normed_two * gain_two).astype(jnp.bfloat16)
    own_routes = lax.dynamic_slice_in_dim(routes, tp_index * row_count, row_count, 0)
    chances = jax.nn.softmax(
        jnp.dot(scaled_two, router, preferred_element_type=jnp.float32), axis=-1
    )
    own_hot = (own_routes[:, None] == expert_ids[None, :]).astype(jnp.float32)
    gate_val = jnp.sum(chances * own_hot, axis=-1, keepdims=True)
    rows_two = lax.all_gather(scaled_two, "tp", axis=0, tiled=True)
    kept_mask = slots >= 0
    places = routes * CAP + slots
    target = jnp.where(kept_mask, places, slot_count)
    slot_owner = jnp.zeros((slot_count + 1,), jnp.int32).at[target].set(positions)[:slot_count]
    filled = jnp.zeros((slot_count + 1,), jnp.bfloat16).at[target].set(1.0)[:slot_count]
    buffer = (rows_two[slot_owner] * filled[:, None]).reshape(expert_count, CAP, model_width)
    inner_full, outer_full = (
        lax.all_gather(w_in, "fsdp", axis=1, tiled=True),
        lax.all_gather(w_out, "fsdp", axis=2, tiled=True),
    )
    pre_act = jnp.einsum("ecd,edf->ecf", buffer, inner_full, preferred_element_type=jnp.float32)
    activated = jax.nn.gelu(pre_act).astype(jnp.bfloat16)
    expert_rows = jnp.einsum(
        "ecf,efd->ecd", activated, outer_full, preferred_element_type=jnp.float32
    ).reshape(slot_count, model_width)
    slot_pick = jnp.where(kept_mask, places, 0)
    kept_col = kept_mask.astype(jnp.float32)[:, None]
    expert_part = expert_rows[slot_pick] * kept_col
    expert_val = lax.psum_scatter(expert_part, "tp", scatter_dimension=0, tiled=True)
    result = hidden + gate_val * expert_val
    grad_out = cotangent.astype(jnp.float32)
    grad_gate = jnp.sum(grad_out * expert_val, axis=-1, keepdims=True)
    grad_expert = (gate_val * grad_out).astype(jnp.bfloat16)
    grad_rows = lax.all_gather(grad_expert, "tp", axis=0, tiled=True)
    grad_slots = (grad_rows[slot_owner] * filled[:, None]).reshape(expert_count, CAP, model_width)
    inner_back, outer_back = (
        lax.all_gather(w_in, "fsdp", axis=1, tiled=True),
        lax.all_gather(w_out, "fsdp", axis=2, tiled=True),
    )
    grad_act = jnp.einsum(
        "ecd,efd->ecf", grad_slots, outer_back, preferred_element_type=jnp.float32
    )
    gelu_back = jax.vjp(jax.nn.gelu, pre_act)[1]
    grad_pre = gelu_back(grad_act)[0].astype(jnp.bfloat16)
    grad_outer = jnp.einsum(
        "ecf,ecd->def", activated, grad_slots, preferred_element_type=jnp.float32
    )
    grad_inner = jnp.einsum("ecd,ecf->def", buffer, grad_pre, preferred_element_type=jnp.float32)
    grad_buffer = jnp.einsum(
        "ecf,edf->ecd", grad_pre, inner_back, preferred_element_type=jnp.float32
    ).reshape(slot_count, model_width)
    grad_two_part = grad_buffer[slot_pick] * kept_col
    grad_logits = (grad_gate * gate_val * (own_hot - chances)).astype(jnp.bfloat16)
    grad_router = jnp.einsum(
        "td,te->de", scaled_two, grad_logits, preferred_element_type=jnp.float32
    )
    grad_scaled_two = lax.psum_scatter(
        grad_two_part, "tp", scatter_dimension=0, tiled=True
    ) + jnp.einsum("te,de->td", grad_logits, router, preferred_element_type=jnp.float32)
    grad_gain_two = jnp.sum(grad_scaled_two * normed_two, axis=0)
    grad_hidden = grad_out + rms_back(grad_scaled_two * gain_two, normed_two, inverse_two)
    grad_attn = lax.all_gather(grad_hidden.astype(jnp.bfloat16), "tp", axis=0, tiled=True)
    grad_output_w = jnp.einsum(
        "tf,td->df", mixed_out, grad_attn, preferred_element_type=jnp.float32
    )
    grad_mixed = (
        jnp.einsum("td,fd->tf", grad_attn, output_full, preferred_element_type=jnp.float32)
        .astype(jnp.bfloat16)
        .reshape(group_rows, head_count, HD)
    )

    def attend_back(carry_in, block_in):
        grad_keys, grad_values, offset_sums = carry_in
        first_row, log_total = block_in
        scores, query_blk = block_scores()
        weights_f = jnp.exp(scores - log_total[..., None])
        grad_weights = jnp.einsum(
            "qhd,khd->hqk", grad_mixed, value_heads, preferred_element_type=jnp.float32
        )
        grad_scores = (
            weights_f * (grad_weights - jnp.sum(weights_f * grad_weights, axis=-1, keepdims=True))
        ).astype(jnp.bfloat16)
        grad_query_blk = (
            jnp.einsum("hqk,khd->qhd", grad_scores, key_heads, preferred_element_type=jnp.float32)
            * score_scale
        )
        grad_keys = (
            grad_keys
            + jnp.einsum("hqk,qhd->khd", grad_scores, query_blk, preferred_element_type=jnp.float32)
            * score_scale
        )
        grad_values = grad_values + jnp.einsum(
            "hqk,qhd->khd",
            weights_f.astype(jnp.bfloat16),
            grad_mixed,
            preferred_element_type=jnp.float32,
        )
        diag_sums = diagonal_sums(grad_scores.astype(jnp.float32))
        window = offset_sums
        offset_sums = window + diag_sums
        return ((grad_keys, grad_values, offset_sums), grad_query_blk)

    start_state = (
        jnp.zeros((group_rows, head_count, HD), jnp.float32),
        jnp.zeros((group_rows, head_count, HD), jnp.float32),
        jnp.zeros((head_count, 2 * group_rows - 1), jnp.float32),
    )
    (grad_keys, grad_values, offset_sums), grad_query_blocks = lax.scan(
        attend_back, start_state, (block_starts, log_totals)
    )
    grad_queries = grad_query_blocks.reshape(group_rows, head_count * HD).astype(jnp.bfloat16)
    grad_keys_low = grad_keys.reshape(group_rows, head_count * HD).astype(jnp.bfloat16)
    grad_values_low = grad_values.reshape(group_rows, head_count * HD).astype(jnp.bfloat16)
    per_offset = offset_sums[:, group_rows - max_len : group_rows + max_len - 1]
    grad_table_here = jnp.dot(per_offset, bucket_hot, precision=HIGHEST).T
    table_full = lax.dynamic_update_slice_in_dim(
        jnp.zeros((bucket_count, head_count * lax.axis_size("tp")), jnp.float32),
        grad_table_here,
        tp_index * head_count,
        1,
    )
    grad_query_w = jnp.einsum(
        "td,tf->df", rows_one, grad_queries, preferred_element_type=jnp.float32
    )
    grad_key_w = jnp.einsum(
        "td,tf->df", rows_one, grad_keys_low, preferred_element_type=jnp.float32
    )
    grad_value_w = jnp.einsum(
        "td,tf->df", rows_one, grad_values_low, preferred_element_type=jnp.float32
    )
    grad_one_part = jnp.einsum(
        "tf,df->td", grad_queries, query_full, preferred_element_type=jnp.float32
    )
    grad_one_part = grad_one_part + jnp.einsum(
        "tf,df->td", grad_keys_low, key_full, preferred_element_type=jnp.float32
    )
    grad_one_part = grad_one_part + jnp.einsum(
        "tf,df->td", grad_values_low, value_full, preferred_element_type=jnp.float32
    )
    grad_scaled_one = lax.psum_scatter(grad_one_part, "tp", scatter_dimension=0, tiled=True)
    grad_gain_one = jnp.sum(grad_scaled_one * normed_one, axis=0)
    grad_inputs = grad_hidden + rms_back(grad_scaled_one * gain_one, normed_one, inverse_one)
    weight_sums = (
        lax.psum_scatter(grad_query_w, "fsdp", scatter_dimension=0, tiled=True),
        lax.psum_scatter(grad_key_w, "fsdp", scatter_dimension=0, tiled=True),
        lax.psum_scatter(grad_value_w, "fsdp", scatter_dimension=0, tiled=True),
        lax.psum_scatter(grad_output_w, "fsdp", scatter_dimension=0, tiled=True),
        lax.psum_scatter(grad_inner, "fsdp", scatter_dimension=0, tiled=True),
        lax.psum_scatter(grad_outer, "fsdp", scatter_dimension=0, tiled=True),
    )
    small_sums = lax.psum((grad_gain_one, grad_gain_two, grad_router, table_full), ("fsdp", "tp"))
    grad_table = lax.dynamic_slice_in_dim(small_sums[3], tp_index * head_count, head_count, 1)
    grad_output_shard = weight_sums[3].T
    grad_inner_shard = jnp.transpose(weight_sums[4], (1, 0, 2))
    grad_outer_shard = jnp.transpose(weight_sums[5], (1, 2, 0))
    return (
        result.astype(jnp.bfloat16),
        grad_inputs,
        small_sums[0],
        small_sums[1],
        weight_sums[0],
        weight_sums[1],
        weight_sums[2],
        grad_output_shard,
        grad_table,
        small_sums[2],
        grad_inner_shard,
        grad_outer_shard,
    )


def solution(mesh):
    placed = (
        P(("fsdp", "tp"), None),
        P(("fsdp", "tp"), None),
        P(),
        P(),
        P("fsdp", "tp"),
        P("fsdp", "tp"),
        P("fsdp", "tp"),
        P("tp", "fsdp"),
        P(None, "tp"),
        P(),
        P(None, "fsdp", "tp"),
        P(None, "tp", "fsdp"),
        P("fsdp", None),
        P("fsdp"),
        P("fsdp"),
        P(),
    )
    return jax.shard_map(
        on_device,
        mesh=mesh,
        in_specs=placed,
        out_specs=(
            P(("fsdp", "tp"), None),
            P(("fsdp", "tp"), None),
            P(),
            P(),
            P("fsdp", "tp"),
            P("fsdp", "tp"),
            P("fsdp", "tp"),
            P("tp", "fsdp"),
            P(None, "tp"),
            P(),
            P(None, "fsdp", "tp"),
            P(None, "tp", "fsdp"),
        ),
        check_vma=False,
    )
```

profile of v0, /device:TPU:0, one launch (start us, length us, event | category | flops | bytes accessed | tf_op | source)
XLA Modules:
  0.0 1756.1 jit_solution(617220329749074706)
XLA Ops:
  13.6 46.2 %all_gather.35 = bf16[768,384]{1,0:T(8,128)(2,1)S(1)} all-gather(bf16[48,384]{1,0:T(8,128)(2,1)} %param.21), channel_id=1, replica_groups=mesh['fsdp'=16,'tp'=2] {'fsdp'}, dimensions={0}, use_global_device_ids=true | all-gather | bytes 626688 | tf_op jit(solution)/shard_map/all_gather | solution.py:80
  73.3 19.2 %reshape.299 = f32[3148794]{0:T(1024)} reshape(f32[6,513,1023]{2,1,0:T(8,128)} %tile.24) | data formatting | bytes 25190352
  92.5 17.4 tile.25
  109.9 11.3 slice.41
  121.2 17.6 %copy.65 = f32[1,6,512,1024]{3,2,1,0:T(8,128)} copy(f32[1,6,512,1024]{3,1,2,0:T(8,128)} %bitcast.90) | data formatting | bytes 25165824
  152.4 51.0 %rev.10 = f32[6,512,512]{1,2,0:T(8,128)} reverse(f32[6,512,512]{1,2,0:T(8,128)} %copy.60), dimensions={1} | reverse | bytes 12582912 | tf_op jit(solution)/shard_map/while/body/eval_jaxpr/rev | solution.py:38
  203.3 39.2 %all_gather.34 = bf16[768,384]{1,0:T(8,128)(2,1)S(1)} all-gather(bf16[48,384]{1,0:T(8,128)(2,1)S(1)} %copy-done.52), channel_id=1, replica_groups=mesh['fsdp'=16,'tp'=2] {'fsdp'}, dimensions={0}, use_global_device_ids=true | all-gather | bytes 626688 | tf_op jit(solution)/shard_map/all_gather | solution.py:79
  244.5 42.0 %all_gather.33 = bf16[768,384]{1,0:T(8,128)(2,1)S(1)} all-gather(bf16[48,384]{1,0:T(8,128)(2,1)S(1)} %copy-done.53), channel_id=1, replica_groups=mesh['fsdp'=16,'tp'=2] {'fsdp'}, dimensions={0}, use_global_device_ids=true | all-gather | bytes 626688 | tf_op jit(solution)/shard_map/all_gather | solution.py:81
  287.0 39.4 %all_gather.36 = bf16[384,768]{0,1:T(8,128)(2,1)S(1)} all-gather(bf16[384,48]{0,1:T(8,128)(2,1)S(1)} %copy-done.54), channel_id=1, replica_groups=mesh['fsdp'=16,'tp'=2] {'fsdp'}, dimensions={1}, use_global_device_ids=true | all-gather | bytes 626688 | tf_op jit(solution)/shard_map/all_gather | solution.py:82
  352.1 106.8 %all-gather.3.cloned.1.call-done = bf16[4,768,1536]{2,1,0:T(8,128)(2,1)} async-done(((bf16[4,48,1536]{2,1,0:T(8,128)(2,1)}), bf16[4,768,1536]{2,1,0:T(8,128)(2,1)}) %all-gather.3.cloned.1.call-update) | async-done | bytes 9437200 | tf_op jit(solution)/shard_map/all_gather | solution.py:147
  466.8 115.4 %all-gather.5.cloned.1.call-done = bf16[4,1536,768]{1,2,0:T(8,128)(2,1)} async-done(((bf16[4,1536,48]{1,2,0:T(8,128)(2,1)}), bf16[4,1536,768]{1,2,0:T(8,128)(2,1)}) %all-gather.5.cloned.1.call-update) | async-done | bytes 9437200 | tf_op jit(solution)/shard_map/all_gather | solution.py:148
  664.0 11.7 convolution_bitcast_fusion.1
  675.7 22.6 %copy.54 = f32[768,4,1536]{2,1,0:T(4,128)} copy(f32[768,4,1536]{0,2,1:T(8,128)} %convolution_bitcast_fusion.1) | data formatting | bytes 37748736 | tf_op jit(solution)/shard_map/ecd,ecf->def/transpose | solution.py:177
  710.6 11.9 convolution_bitcast_fusion
  725.9 34.8 %rev.11 = f32[6,512,512]{1,2,0:T(8,128)} reverse(bf16[6,512,512]{1,2,0:T(8,128)(2,1)S(1)} %multiply_convert_fusion), dimensions={1} | reverse | bytes 9437184 | tf_op jit(solution)/shard_map/while/body/eval_jaxpr/rev | solution.py:29
  776.7 18.3 %copy.63 = f32[1,6,512,1024]{3,1,2,0:T(8,128)} copy(f32[1,6,512,1024]{3,2,1,0:T(8,128)} %pad_bitcast_fusion) | data formatting | bytes 25165824
  795.0 11.5 slice.43
  806.5 12.5 reshape.301
  819.1 14.4 reshape.231
  841.4 44.2 %all-reduce.2 = (f32[768]{0:T(1024)}, f32[768]{0:T(1024)}, f32[32,12]{0,1:T(8,128)S(1)}, f32[768,4]{0,1:T(4,128)}) all-reduce(f32[768]{0:T(1024)S(1)} %get-tuple-element.122, f32[768]{0:T(1024)S(1)} %copy-done.63, f32[32,12]{0,1:T(8,128)S(1)} %dynamic_update_slice.11, ...), channel_id=1, replica_groups=mesh['fsdp'=16,'tp'=2] {'fsdp','tp'}, use_global_device_ids=true, to_apply=%region_20.21 | all-reduce | flops 4992 | bytes 39936 | tf_op jit(solution)/shard_map/psum | solution.py:280
  888.9 326.9 %all-reduce.5.cloned.1.call-done = f32[768,4,1536]{2,1,0:T(4,128)} async-done(((f32[768,4,1536]{2,1,0:T(4,128)}), f32[768,4,1536]{2,1,0:T(4,128)}) %all-reduce.5.cloned.1.call-update) | async-done | bytes 18874384
  1218.5 111.0 %reduce-scatter.22.cloned.1.call-done = f32[48,384]{1,0:T(8,128)} async-done(((f32[768,384]{1,0:T(8,128)}), f32[48,384]{1,0:T(8,128)}) %reduce-scatter.22.cloned.1.call-update) | async-done | bytes 73744 | tf_op jit(solution)/shard_map/reduce_scatter | solution.py:275
  1329.5 127.9 %reduce-scatter.24.cloned.1.call-done = f32[48,384]{1,0:T(8,128)} async-done(((f32[768,384]{1,0:T(8,128)}), f32[48,384]{1,0:T(8,128)}) %reduce-scatter.24.cloned.1.call-update) | async-done | bytes 73744 | tf_op jit(solution)/shard_map/reduce_scatter | solution.py:276
  1457.4 290.9 %reduce-scatter.26.cloned.1.call-done = f32[48,4,1536]{2,0,1:T(8,128)} async-done(((f32[768,4,1536]{2,0,1:T(8,128)}), f32[48,4,1536]{2,0,1:T(8,128)}) %reduce-scatter.26.cloned.1.call-update) | async-done | bytes 1179664 | tf_op jit(solution)/shard_map/reduce_scatter | solution.py:278
  (286 shorter events, 194.0 us)
Async XLA Ops:
  8.0 588.2 %copy-start = (bf16[768,4]{0,1:T(4,128)(2,1)S(1)}, bf16[768,4]{0,1:T(4,128)(2,1)}, u32[]{:S(2)}) copy-start(bf16[768,4]{0,1:T(4,128)(2,1)} %param.25) | copy-start | bytes 18436
  8.0 58.7 %copy-start.80 = (bf16[32,6]{0,1:T(8,128)(2,1)S(1)}, bf16[32,6]{0,1:T(8,128)(2,1)}, u32[]{:S(2)}) copy-start(bf16[32,6]{0,1:T(8,128)(2,1)} %param.24) | copy-start | bytes 1156
  8.0 336.9 %reduce-scatter.10.cloned.1.call-start = ((), (), s32[]{:S(2)}) async-start(), calls=%async_computation.9 | async-start | bytes 2359296 | tf_op jit(solution)/shard_map/reduce_scatter | solution.py:129
  13.6 272.9 %copy-start.9 = (bf16[512,768]{1,0:T(8,128)(2,1)}, bf16[512,768]{1,0:T(8,128)(2,1)S(1)}, u32[]{:S(2)}) copy-start(bf16[512,768]{1,0:T(8,128)(2,1)S(1)} %all_gather.32) | copy-start | bytes 2359300
  59.8 182.7 %copy-start.23 = (bf16[768,384]{1,0:T(8,128)(2,1)}, bf16[768,384]{1,0:T(8,128)(2,1)S(1)}, u32[]{:S(2)}) copy-start(bf16[768,384]{1,0:T(8,128)(2,1)S(1)} %all_gather.35) | copy-start | bytes 1769476
  152.4 91.6 %copy-start.81 = (s32[1,4]{1,0:T(1,128)S(1)}, s32[1,4]{1,0:T(1,128)}, u32[]{:S(2)}) copy-start(s32[1,4]{1,0:T(1,128)} %param.28) | copy-start | bytes 52
  152.4 92.1 %copy-start.53 = (bf16[48,384]{1,0:T(8,128)(2,1)S(1)}, bf16[48,384]{1,0:T(8,128)(2,1)}, u32[]{:S(2)}) copy-start(bf16[48,384]{1,0:T(8,128)(2,1)} %param.22) | copy-start | bytes 110596
  203.3 83.7 %copy-start.54 = (bf16[384,48]{0,1:T(8,128)(2,1)S(1)}, bf16[384,48]{0,1:T(8,128)(2,1)}, u32[]{:S(2)}) copy-start(bf16[384,48]{0,1:T(8,128)(2,1)} %param.23) | copy-start | bytes 110596
  243.4 87.4 %copy-start.34 = (bf16[512,384]{0,1:T(8,128)(2,1)}, bf16[512,384]{0,1:T(8,128)(2,1)S(1)}, u32[]{:S(2)}) copy-start(bf16[512,384]{0,1:T(8,128)(2,1)S(1)} %convolution_convert_fusion.1) | copy-start | bytes 1179652
  243.9 86.9 %copy-start.32 = (bf16[512,384]{0,1:T(8,128)(2,1)}, bf16[512,384]{0,1:T(8,128)(2,1)S(1)}, u32[]{:S(2)}) copy-start(bf16[512,384]{0,1:T(8,128)(2,1)S(1)} %convolution_convert_fusion.2) | copy-start | bytes 1179652
  336.2 122.7 %all-gather.3.cloned.1.call-start = ((), (), s32[]{:S(2)}) async-start(), calls=%async_computation.10 | async-start | bytes 10027008 | tf_op jit(solution)/shard_map/all_gather | solution.py:147
  336.7 245.4 %all-gather.5.cloned.1.call-start = ((), (), s32[]{:S(2)}) async-start(), calls=%async_computation.11 | async-start | bytes 10027008 | tf_op jit(solution)/shard_map/all_gather | solution.py:148
  337.3 266.2 %reduce-scatter.12.cloned.1.call-start = ((), (), s32[]{:S(2)}) async-start(), calls=%async_computation.12 | async-start | bytes 2359296 | tf_op jit(solution)/shard_map/reduce_scatter | solution.py:158
  346.3 301.0 %copy-start.6 = (f32[256,768]{1,0:T(8,128)}, f32[256,768]{1,0:T(8,128)S(1)}, u32[]{:S(2)}) copy-start(f32[256,768]{1,0:T(8,128)S(1)} %get-tuple-element.129) | copy-start | bytes 2359300
  352.0 114.7 %copy-start.8 = (bf16[768,768]{1,0:T(8,128)(2,1)}, bf16[768,768]{1,0:T(8,128)(2,1)S(1)}, u32[]{:S(2)}) copy-start(bf16[768,768]{1,0:T(8,128)(2,1)S(1)} %gather_fusion.1) | copy-start | bytes 3538948
  596.1 49.0 %reduce-scatter.14.cloned.1.call-start = ((), (), s32[]{:S(2)}) async-start(), calls=%async_computation.13 | async-start | bytes 2359296 | tf_op jit(solution)/shard_map/reduce_scatter | solution.py:186
  634.7 205.1 %reduce-scatter.16.cloned.1.call-start = ((), (), s32[]{:S(2)}) async-start(), calls=%async_computation.14 | async-start | bytes 2359296 | tf_op jit(solution)/shard_map/reduce_scatter | solution.py:269
  663.9 551.8 %all-reduce.5.cloned.1.call-start = ((), (), s32[]{:S(2)}) async-start(), calls=%async_computation.20 | async-start | bytes 37748736
  698.4 520.1 %reduce-scatter.18.cloned.1.call-start = ((), (), s32[]{:S(2)}) async-start(), calls=%async_computation.15 | async-start | bytes 1253376 | tf_op jit(solution)/shard_map/reduce_scatter | solution.py:273
  701.3 517.2 %reduce-scatter.20.cloned.1.call-start = ((), (), s32[]{:S(2)}) async-start(), calls=%async_computation.16 | async-start | bytes 1253376 | tf_op jit(solution)/shard_map/reduce_scatter | solution.py:274
  704.3 625.3 %reduce-scatter.22.cloned.1.call-start = ((), (), s32[]{:S(2)}) async-start(), calls=%async_computation.17 | async-start | bytes 1253376 | tf_op jit(solution)/shard_map/reduce_scatter | solution.py:275
  707.6 749.9 %reduce-scatter.24.cloned.1.call-start = ((), (), s32[]{:S(2)}) async-start(), calls=%async_computation.18 | async-start | bytes 1253376 | tf_op jit(solution)/shard_map/reduce_scatter | solution.py:276
  710.5 1037.8 %reduce-scatter.26.cloned.1.call-start = ((), (), s32[]{:S(2)}) async-start(), calls=%async_computation.19 | async-start | bytes 20054016 | tf_op jit(solution)/shard_map/reduce_scatter | solution.py:278
  886.1 862.2 %copy-start.1 = (bf16[768,4]{0,1:T(4,128)(2,1)S(1)}, bf16[768,4]{0,1:T(4,128)(2,1)}, u32[]{:S(2)}) copy-start(bf16[768,4]{0,1:T(4,128)(2,1)} %param.25) | copy-start | bytes 18436
  (72 other events, 1016.4 us)
Sparse Core Ops, SparseCore 0:
  336.3 6.0 reduce-scatter.9
  596.2 7.2 reduce-scatter.11
  634.8 10.2 reduce-scatter.13
  664.0 10.2 reduce-scatter.15
  704.2 260.0 reduce-scatter.17
  969.5 228.0 reduce-scatter.19
  1203.0 126.5 reduce-scatter.21
  1334.9 122.5 reduce-scatter.23
  1464.8 283.5 reduce-scatter.25
Sparse Core Ops, SparseCore 1:
  339.7 119.1 all-gather.2
  461.8 120.3 all-gather.4
  698.5 517.2 all-reduce.4
where the time goes:
time: 1770 us; the launch traced here: 1760 us
  waiting for transfers between devices  1100 us (62%)
  local copies, waits for them, and re-layouts  299 us (17%)
  blocking collectives  221 us (12%)
  matrix products  93.4 us (5%)
  other arithmetic  27.3 us (2%)
  between operations  17.8 us (1%)
    unnamed x13, waiting for transfers between devices  328 us
    reduce_scatter x1, waiting for transfers between devices, on_device(): lax.psum_scatter(grad_outer, 'fsdp', scatter_dimension=0, tiled=True)  291 us
    reduce_scatter x1, waiting for transfers between devices, on_device(): lax.psum_scatter(grad_output_w, 'fsdp', scatter_dimension=0, tiled=True)  128 us
    all_gather x1, waiting for transfers between devices, on_device(): lax.all_gather(w_out, 'fsdp', axis=2, tiled=True)  115 us
    reduce_scatter x1, waiting for transfers between devices, on_device(): lax.psum_scatter(grad_value_w, 'fsdp', scatter_dimension=0, tiled=True)  111 us
    all_gather x1, waiting for transfers between devices, on_device(): lax.all_gather(w_in, 'fsdp', axis=1, tiled=True)  107 us
    unnamed x177, local copies, waits for them, and re-layouts  96.3 us
    rev x1, local copies, waits for them, and re-layouts, toeplitz_block(): return skewed[:, ::-1, :]  51 us
  transfers between devices with their start and end apart: 12, of which 8 were waited for; matrix products, arithmetic and copies ran while one was open for 12% of the time, Pallas kernels for 0%

commit v1 on v0

v1 whole, which is shorter than its diff:
```python
import functools
import math

import jax
import jax.numpy as jnp
from jax import lax
from jax.experimental import pallas as pl
from jax.experimental.pallas import tpu as pltpu
from jax.sharding import PartitionSpec as P

HD = 64
CAP = 192
EPSILON = 1e-06
MASKED = -1e30
HIGHEST = lax.Precision.HIGHEST
F32 = jnp.float32
BF16 = jnp.bfloat16
NT = (((1,), (1,)), ((), ()))
TN = (((0,), (0,)), ((), ()))


def rms_stats(values):
    inverse = lax.rsqrt(jnp.mean(values * values, axis=-1, keepdims=True) + EPSILON)
    return (values * inverse, inverse)


def rms_back(grad_hat, normed, inverse):
    return inverse * (grad_hat - normed * jnp.mean(grad_hat * normed, axis=-1, keepdims=True))


def tp_swap(values):
    return lax.ppermute(values, "tp", [(0, 1), (1, 0)])


def tp_gather(values):
    other = tp_swap(values)
    first = lax.axis_index("tp") == 0
    low = jnp.where(first, values, other)
    high = jnp.where(first, other, values)
    return jnp.concatenate([low, high], axis=0)


def tp_scatter(values):
    half = values.shape[0] // 2
    me = lax.axis_index("tp")
    away = lax.dynamic_slice_in_dim(values, (1 - me) * half, half, 0)
    keep = lax.dynamic_slice_in_dim(values, me * half, half, 0)
    return keep + tp_swap(away)


def fsdp_gather(shard):
    return lax.all_gather(shard, "fsdp", axis=0, tiled=False)


def add_low(left, right):
    return (left.astype(F32) + right.astype(F32)).astype(BF16)


def scatter_grid(blocks):
    index = lax.axis_index("fsdp")
    z_at, y_at, x_at = index // 4, (index // 2) % 2, index % 2
    grid = blocks.reshape((4, 2, 2) + blocks.shape[1:])
    half = blocks.shape[1] // 2

    def flip(values, bit):
        return lax.ppermute(values, "fsdp", [(i, i ^ bit) for i in range(16)])

    def fold(part, place, axis, bit):
        away = lax.dynamic_index_in_dim(part, 1 - place, axis, False)
        keep = lax.dynamic_index_in_dim(part, place, axis, False)
        return add_low(keep, flip(away, bit))

    first = fold(fold(grid[:, :, :, :half], x_at, 2, 1), y_at, 1, 2)
    second = fold(fold(grid[:, :, :, half:], y_at, 1, 2), x_at, 1, 1)
    column = jnp.concatenate([first, second], axis=1)

    def pick(target):
        return lax.dynamic_index_in_dim(column, jnp.clip(target, 0, 3), 0, False)

    rising = falling = None
    for offset in (3, 2, 1):
        up, down = pick(z_at + offset), pick(z_at - offset)
        if rising is not None:
            up, down = add_low(up, rising), add_low(down, falling)
        rising = lax.ppermute(
            up, "fsdp", [(i, i + 4) for i in range(12) if i // 4 + offset <= 3]
        )
        falling = lax.ppermute(
            down, "fsdp", [(i, i - 4) for i in range(4, 16) if i // 4 - offset >= 0]
        )
    return pick(z_at).astype(F32) + rising.astype(F32) + falling.astype(F32)


def fsdp_scatter(blocks):
    if USE_GRID and blocks.shape[0] == 16:
        return scatter_grid(blocks.astype(BF16))
    low = blocks.astype(BF16)
    flat = low.reshape((-1, low.shape[-1]))
    return lax.psum_scatter(flat, "fsdp", scatter_dimension=0, tiled=True).astype(F32).reshape(
        blocks.shape[1:]
    )


def head_weights(query, key, window, same, rows):
    scale = 1.0 / math.sqrt(HD)
    skew = pltpu.roll(
        jnp.broadcast_to(window, (rows, rows)), 0, 1, stride=1, stride_axis=0
    )
    scores = lax.dot_general(query, key, NT, preferred_element_type=F32) * scale + skew
    scores = jnp.where(same, scores, MASKED)
    raised = jnp.exp(scores - jnp.max(scores, axis=-1, keepdims=True))
    return raised / jnp.sum(raised, axis=-1, keepdims=True)


def attend_kernel(q_ref, k_ref, v_ref, win_ref, col_ref, row_ref, o_ref):
    rows = q_ref.shape[0]
    same = col_ref[...] == row_ref[...]
    mixed = []
    for head in range(2):
        part = slice(head * HD, (head + 1) * HD)
        weights = head_weights(
            q_ref[:, part], k_ref[:, part], win_ref[0, head : head + 1, :], same, rows
        )
        mixed.append(
            jnp.dot(weights.astype(BF16), v_ref[:, part], preferred_element_type=F32)
        )
    o_ref[...] = jnp.concatenate(mixed, axis=1).astype(BF16)


def attend_back_kernel(
    q_ref, k_ref, v_ref, do_ref, win_ref, col_ref, row_ref, dq_ref, dk_ref, dv_ref, sums_ref
):
    rows = q_ref.shape[0]
    scale = 1.0 / math.sqrt(HD)
    same = col_ref[...] == row_ref[...]
    all_dq, all_dk, all_dv, all_sums = [], [], [], []
    for head in range(2):
        part = slice(head * HD, (head + 1) * HD)
        query, key, value, grad = q_ref[:, part], k_ref[:, part], v_ref[:, part], do_ref[:, part]
        weights = head_weights(query, key, win_ref[0, head : head + 1, :], same, rows)
        low = weights.astype(BF16)
        grad_weights = lax.dot_general(grad, value, NT, preferred_element_type=F32)
        inner = jnp.sum(weights * grad_weights, axis=-1, keepdims=True)
        grad_scores = (weights * (grad_weights - inner)).astype(BF16)
        all_dq.append(jnp.dot(grad_scores, key, preferred_element_type=F32) * scale)
        all_dk.append(
            lax.dot_general(grad_scores, query, TN, preferred_element_type=F32) * scale
        )
        all_dv.append(lax.dot_general(low, grad, TN, preferred_element_type=F32))
        fold = grad_scores.astype(F32)
        count = rows
        while count > 8:
            count //= 2
            fold = fold[:count] + pltpu.roll(fold[count:], rows - count, 1)
        total = fold[0:1]
        for line in range(1, 8):
            total = total + pltpu.roll(fold, rows - line, 1)[line : line + 1]
        all_sums.append(total)
    dq_ref[...] = jnp.concatenate(all_dq, axis=1).astype(BF16)
    dk_ref[...] = jnp.concatenate(all_dk, axis=1).astype(BF16)
    dv_ref[...] = jnp.concatenate(all_dv, axis=1).astype(BF16)
    sums_ref[0] = jnp.concatenate(all_sums, axis=0)


def attend_call(kernel, wide_out, sums_out, wide_in, window, seg_col, seg_row):
    rows, width = wide_in[0].shape
    steps = width // (2 * HD)
    wide = pl.BlockSpec((rows, 2 * HD), lambda i: (0, i))
    lines = pl.BlockSpec((1, 2, rows), lambda i: (i, 0, 0))
    flops = 2 * 2 * rows * rows * width * (2 if wide_out == 1 else 5)
    return pl.pallas_call(
        kernel,
        grid=(steps,),
        in_specs=[wide] * len(wide_in)
        + [
            lines,
            pl.BlockSpec((rows, 1), lambda i: (0, 0)),
            pl.BlockSpec((1, rows), lambda i: (0, 0)),
        ],
        out_specs=[wide] * wide_out + [lines] * sums_out,
        out_shape=[jax.ShapeDtypeStruct((rows, width), BF16)] * wide_out
        + [jax.ShapeDtypeStruct((steps, 2, rows), F32)] * sums_out,
        cost_estimate=pl.CostEstimate(
            flops=flops, bytes_accessed=2 * rows * width * 8, transcendentals=rows * rows * 6
        ),
        compiler_params=pltpu.CompilerParams(vmem_limit_bytes=48 * 1024 * 1024),
    )(*wide_in, window, seg_col, seg_row)


def on_device(
    tokens,
    cotangent,
    gain_attn,
    gain_moe,
    w_query,
    w_key,
    w_value,
    w_output,
    bias_table,
    router,
    w_in,
    w_out,
    lengths,
    routes,
    slots,
    buckets,
):
    row_count, model_width = tokens.shape
    group_rows = routes.shape[0]
    bucket_count, head_count = bias_table.shape
    expert_count = router.shape[1]
    slot_count = expert_count * CAP
    hidden_width = w_in.shape[2]
    head_width = w_query.shape[1]
    shard_rows = w_query.shape[0]
    n_fsdp = lax.axis_size("fsdp")
    span_len = buckets.shape[0]
    max_len = (span_len + 1) // 2
    tp_index = lax.axis_index("tp")
    positions = jnp.arange(group_rows, dtype=jnp.int32)
    expert_ids = jnp.arange(expert_count, dtype=jnp.int32)

    attn_shard = jnp.stack([w_query, w_key, w_value, w_output.T])
    attn_all = fsdp_gather(attn_shard)
    inner_all = fsdp_gather(w_in)
    outer_all = fsdp_gather(jnp.transpose(w_out, (0, 2, 1)))
    attn_full = jnp.transpose(attn_all, (1, 0, 2, 3)).reshape(4, model_width, head_width)
    inner_full = jnp.transpose(inner_all, (1, 0, 2, 3)).reshape(
        expert_count, model_width, hidden_width
    )
    outer_full = jnp.transpose(outer_all, (1, 0, 2, 3)).reshape(
        expert_count, model_width, hidden_width
    )

    inputs = tokens.astype(F32)
    gain_one = gain_attn.astype(F32)
    gain_two = gain_moe.astype(F32)
    normed_one, inverse_one = rms_stats(inputs)
    scaled_one = (normed_one * gain_one).astype(BF16)
    rows_one = tp_gather(scaled_one)

    bounds = jnp.cumsum(lengths[0])
    segment = jnp.sum((positions[:, None] >= bounds[None, :]).astype(jnp.int32), axis=1)
    seg_col, seg_row = segment[:, None], segment[None, :]
    bucket_ids = jnp.arange(bucket_count, dtype=jnp.int32)
    window_buckets = jnp.concatenate(
        [
            buckets[max_len - 1 :],
            jnp.full((group_rows - span_len,), -1, jnp.int32),
            buckets[: max_len - 1],
        ]
    )
    window_hot = (window_buckets[:, None] == bucket_ids[None, :]).astype(F32)
    window = jnp.dot(window_hot, bias_table.astype(F32), precision=HIGHEST).T.reshape(
        head_count // 2, 2, group_rows
    )

    queries, keys_all, values_all = (
        jnp.dot(rows_one, attn_full[i], preferred_element_type=F32).astype(BF16) for i in range(3)
    )
    (mixed_out,) = attend_call(
        attend_kernel, 1, 0, (queries, keys_all, values_all), window, seg_col, seg_row
    )
    attn_part = lax.dot_general(mixed_out, attn_full[3], NT, preferred_element_type=F32)
    hidden = inputs + tp_scatter(attn_part)
    normed_two, inverse_two = rms_stats(hidden)
    scaled_two = (normed_two * gain_two).astype(BF16)
    rows_two = tp_gather(scaled_two)

    own_routes = lax.dynamic_slice_in_dim(routes, tp_index * row_count, row_count, 0)
    chances = jax.nn.softmax(jnp.dot(scaled_two, router, preferred_element_type=F32), axis=-1)
    own_hot = (own_routes[:, None] == expert_ids[None, :]).astype(F32)
    gate_val = jnp.sum(chances * own_hot, axis=-1, keepdims=True)

    kept_mask = slots >= 0
    places = jnp.where(kept_mask, routes * CAP + slots, -1)
    slot_ids = jnp.arange(slot_count, dtype=jnp.int32)
    dispatch = (slot_ids[:, None] == places[None, :]).astype(BF16)
    collect = (places[:, None] == slot_ids[None, :]).astype(BF16)

    def to_slots(rows):
        return (
            jnp.dot(dispatch, rows, preferred_element_type=F32)
            .astype(BF16)
            .reshape(expert_count, CAP, model_width)
        )

    def to_tokens(rows):
        high = rows.astype(BF16)
        low = (rows - high.astype(F32)).astype(BF16)
        return jnp.dot(collect, high, preferred_element_type=F32) + jnp.dot(
            collect, low, preferred_element_type=F32
        )

    buffer = to_slots(rows_two)
    pre_act = jnp.einsum("ecd,edf->ecf", buffer, inner_full, preferred_element_type=F32)
    activated = jax.nn.gelu(pre_act).astype(BF16)
    expert_rows = jnp.einsum(
        "ecf,edf->ecd", activated, outer_full, preferred_element_type=F32
    ).reshape(slot_count, model_width)
    expert_val = tp_scatter(to_tokens(expert_rows))
    result = hidden + gate_val * expert_val

    grad_out = cotangent.astype(F32)
    grad_gate = jnp.sum(grad_out * expert_val, axis=-1, keepdims=True)
    grad_expert = (gate_val * grad_out).astype(BF16)
    grad_slots = to_slots(tp_gather(grad_expert))

    def blocked(grads, parts):
        return jnp.transpose(
            grads.astype(BF16).reshape(parts, n_fsdp, shard_rows, grads.shape[-1]), (1, 0, 2, 3)
        )

    grad_outer = jnp.einsum("ecd,ecf->edf", grad_slots, activated, preferred_element_type=F32)
    outer_sum = fsdp_scatter(blocked(grad_outer, expert_count))
    grad_act = jnp.einsum("ecd,edf->ecf", grad_slots, outer_full, preferred_element_type=F32)
    grad_pre = jax.vjp(jax.nn.gelu, pre_act)[1](grad_act)[0].astype(BF16)
    grad_inner = jnp.einsum("ecd,ecf->edf", buffer, grad_pre, preferred_element_type=F32)
    inner_sum = fsdp_scatter(blocked(grad_inner, expert_count))
    grad_buffer = jnp.einsum(
        "ecf,edf->ecd", grad_pre, inner_full, preferred_element_type=F32
    ).reshape(slot_count, model_width)
    grad_logits = (grad_gate * gate_val * (own_hot - chances)).astype(BF16)
    grad_router = jnp.einsum("td,te->de", scaled_two, grad_logits, preferred_element_type=F32)
    grad_scaled_two = tp_scatter(to_tokens(grad_buffer)) + jnp.einsum(
        "te,de->td", grad_logits, router, preferred_element_type=F32
    )
    grad_gain_two = jnp.sum(grad_scaled_two * normed_two, axis=0)
    grad_hidden = grad_out + rms_back(grad_scaled_two * gain_two, normed_two, inverse_two)
    grad_attn = tp_gather(grad_hidden.astype(BF16))
    grad_mixed = jnp.dot(grad_attn, attn_full[3], preferred_element_type=F32).astype(BF16)
    grad_queries, grad_keys, grad_values, window_sums = attend_call(
        attend_back_kernel,
        3,
        1,
        (queries, keys_all, values_all, grad_mixed),
        window,
        seg_col,
        seg_row,
    )
    attn_grads = jnp.stack(
        [
            lax.dot_general(left, right, TN, preferred_element_type=F32)
            for left, right in (
                (rows_one, grad_queries),
                (rows_one, grad_keys),
                (rows_one, grad_values),
                (grad_attn, mixed_out),
            )
        ]
    )
    attn_sum = fsdp_scatter(blocked(attn_grads, 4))
    grad_one_part = sum(
        lax.dot_general(grads, attn_full[i], NT, preferred_element_type=F32)
        for i, grads in enumerate((grad_queries, grad_keys, grad_values))
    )
    grad_scaled_one = tp_scatter(grad_one_part)
    grad_gain_one = jnp.sum(grad_scaled_one * normed_one, axis=0)
    grad_inputs = grad_hidden + rms_back(grad_scaled_one * gain_one, normed_one, inverse_one)

    grad_table_here = jnp.dot(
        window_sums.reshape(head_count, group_rows), window_hot, precision=HIGHEST
    )
    table_full = lax.dynamic_update_slice_in_dim(
        jnp.zeros((head_count * lax.axis_size("tp"), bucket_count), F32),
        grad_table_here,
        tp_index * head_count,
        0,
    )
    pieces = [grad_gain_one, grad_gain_two, grad_router.T.reshape(-1), table_full.reshape(-1)]
    small = lax.psum(jnp.concatenate(pieces), ("fsdp", "tp"))
    split = [0]
    for piece in pieces:
        split.append(split[-1] + piece.shape[0])
    total_one, total_two, total_router, total_table = (
        small[split[i] : split[i + 1]] for i in range(4)
    )
    grad_table = lax.dynamic_slice_in_dim(
        total_table.reshape(-1, bucket_count), tp_index * head_count, head_count, 0
    ).T
    return (
        result.astype(BF16),
        grad_inputs,
        total_one,
        total_two,
        attn_sum[0],
        attn_sum[1],
        attn_sum[2],
        attn_sum[3].T,
        grad_table,
        total_router.reshape(expert_count, model_width).T,
        inner_sum,
        jnp.transpose(outer_sum, (0, 2, 1)),
    )


USE_GRID = True

def solution(mesh):
    placed = (
        P(("fsdp", "tp"), None),
        P(("fsdp", "tp"), None),
        P(),
        P(),
        P("fsdp", "tp"),
        P("fsdp", "tp"),
        P("fsdp", "tp"),
        P("tp", "fsdp"),
        P(None, "tp"),
        P(),
        P(None, "fsdp", "tp"),
        P(None, "tp", "fsdp"),
        P("fsdp", None),
        P("fsdp"),
        P("fsdp"),
        P(),
    )
    return jax.shard_map(
        on_device,
        mesh=mesh,
        in_specs=placed,
        out_specs=(
            P(("fsdp", "tp"), None),
            P(("fsdp", "tp"), None),
            P(),
            P(),
            P("fsdp", "tp"),
            P("fsdp", "tp"),
            P("fsdp", "tp"),
            P("tp", "fsdp"),
            P(None, "tp"),
            P(),
            P(None, "fsdp", "tp"),
            P(None, "tp", "fsdp"),
        ),
        check_vma=False,
    )
```

time: 1770 us -> 772 us (0.44)
  waiting for transfers between devices: 1100 us -> 451 us
  local copies, waits for them, and re-layouts: 299 us -> 76.8 us
  blocking collectives: 221 us -> 38.6 us
  starting transfers between devices: 0.67 us -> 61.7 us
  matrix products: 93.4 us -> 64.6 us
    reduce_scatter x9 -> x0, waiting for transfers between devices: 547 us -> none  [the longest x1 291 us: on_device(): lax.psum_scatter(grad_outer, 'fsdp', scatter_dimension=0, tiled=True)]
    unnamed x13 -> x3, waiting for transfers between devices: 328 us -> 1.39 us
    all_gather x8 -> x0, blocking collectives: 176 us -> none  [the longest x1 46.2 us: on_device(): lax.all_gather(w_key, 'fsdp', axis=0, tiled=True)]
    ppermute x0 -> x38, waiting for transfers between devices: none -> 172 us  [the longest x12 129 us: flip(): return lax.ppermute(values, 'fsdp', [(i, i ^ bit) for i in range(16)])]
    unnamed x177 -> x109, local copies, waits for them, and re-layouts: 96.3 us -> 10.2 us
    rev x2 -> x0, local copies, waits for them, and re-layouts: 85.8 us -> none  [the longest x1 51 us: toeplitz_block(): return skewed[:, ::-1, :]]
    ppermute x0 -> x38, starting transfers between devices: none -> 61.5 us  [the longest x9 36.4 us: scatter_grid(): lax.ppermute(up, 'fsdp', [(i, i + 4) for i in range(12) if i // 4 + offse...]
    all_gather x2 -> x3, waiting for transfers between devices: 222 us -> 277 us  [fsdp_gather(): return lax.all_gather(shard, 'fsdp', axis=0, tiled=False)]
  transfers between devices with their start and end apart: 12 -> 41, of which waited for: 8 -> 20; matrix products, arithmetic and copies ran while one was open for 12% -> 15% of each run, Pallas kernels for 0% -> 2%
where the time goes in v1:
time: 772 us; the launch traced here: 761 us
  waiting for transfers between devices  451 us (58%)
  local copies, waits for them, and re-layouts  76.8 us (10%)
  matrix products  64.6 us (8%)
  starting transfers between devices  61.7 us (8%)
  blocking collectives  38.6 us (5%)
  other arithmetic  36.2 us (5%)
  Pallas kernels  16.7 us (2%)
  between operations  15.3 us (2%)
    all_gather x3, waiting for transfers between devices, fsdp_gather(): return lax.all_gather(shard, 'fsdp', axis=0, tiled=False)  277 us
    ppermute x12, waiting for transfers between devices, flip(): return lax.ppermute(values, 'fsdp', [(i, i ^ bit) for i in range(16)])  129 us
    psum x1, blocking collectives, on_device(): small = lax.psum(jnp.concatenate(pieces), ('fsdp', 'tp'))  38.6 us
    ppermute x9, starting transfers between devices, scatter_grid(): lax.ppermute(up, 'fsdp', [(i, i + 4) for i in range(12) if i // 4 + offse...  36.4 us
    ppermute x9, waiting for transfers between devices, scatter_grid(): lax.ppermute(up, 'fsdp', [(i, i + 4) for i in range(12) if i // 4 + offse...  33.7 us
    pallas_call x2, Pallas kernels, attend_call(): pl.pallas_call(kernel, grid=(steps,), in_specs=[wide] * len(wide_in) + [l...  16.7 us
    reshape x2, local copies, waits for them, and re-layouts, blocked(): grads.astype(BF16).reshape(parts, n_fsdp, shard_rows, grads.shape[-1])  16.2 us
    all_gather x2, local copies, waits for them, and re-layouts, fsdp_gather(): return lax.all_gather(shard, 'fsdp', axis=0, tiled=False)  16.2 us
  transfers between devices with their start and end apart: 41, of which 20 were waited for; matrix products, arithmetic and copies ran while one was open for 15% of the time, Pallas kernels for 2%

profile of v1, /device:TPU:0, one launch (start us, length us, event | category | flops | bytes accessed | tf_op | source)
XLA Modules:
  0.0 760.8 jit_solution(11484576107901017467)
XLA Ops:
  15.5 60.9 %all-gather.7.cloned.1.call-done = bf16[64,48,384]{2,1,0:T(8,128)(2,1)} async-done(((bf16[4,48,384]{2,1,0:T(8,128)(2,1)}), bf16[64,48,384]{2,1,0:T(8,128)(2,1)}) %all-gather.7.cloned.1.call-update) | async-done | bytes 2359312 | tf_op jit(solution)/shard_map/all_gather | solution.py:52
  81.4 8.0 %shard_map.247 = bf16[512,384]{1,0:T(8,128)(2,1)S(1)} custom-call(bf16[512,384]{1,0:T(8,128)(2,1)S(1)} %convolution_convert_fusion.9.q_ref, bf16[512,384]{1,0:T(8,128)(2,1)S(1)} %convolution_convert_fusion.8.k_ref, bf16[512,384]{1,0:T(8,128)(2,1)S(1)} %convolution_convert_fusion.7.v_ref, f32[3,2,512]{2,1,0:T(2,128)S(1)} %reshape.222.win_ref, ...), custom_call_target="tpu_custom_call" | custom-call | flops 805306368 | bytes 3145728 | tf_op jit(solution)/shard_map/pallas_call | solution.py:171
  100.0 100.6 %all-gather.9.cloned.1.call-done = bf16[64,48,1536]{2,1,0:T(8,128)(2,1)} async-done(((bf16[4,48,1536]{2,1,0:T(8,128)(2,1)}), bf16[64,48,1536]{2,1,0:T(8,128)(2,1)}) %all-gather.9.cloned.1.call-update) | async-done | bytes 9437200 | tf_op jit(solution)/shard_map/all_gather | solution.py:52
  200.6 8.1 %copy.57 = bf16[16,4,48,1536]{3,2,0,1:T(8,128)(2,1)} copy(bf16[16,4,48,1536]{3,2,1,0:T(8,128)(2,1)} %bitcast.295) | data formatting | bytes 18874368 | tf_op jit(solution)/shard_map/all_gather | solution.py:52
  208.7 115.4 %all-gather.11.cloned.1.call-done = bf16[64,48,1536]{2,1,0:T(8,128)(2,1)} async-done(((bf16[4,48,1536]{2,1,0:T(8,128)(2,1)}), bf16[64,48,1536]{2,1,0:T(8,128)(2,1)}) %all-gather.11.cloned.1.call-update) | async-done | bytes 9437200 | tf_op jit(solution)/shard_map/all_gather | solution.py:52
  324.1 8.1 %copy.58 = bf16[16,4,48,1536]{3,2,0,1:T(8,128)(2,1)} copy(bf16[16,4,48,1536]{3,2,1,0:T(8,128)(2,1)} %bitcast.296) | data formatting | bytes 18874368 | tf_op jit(solution)/shard_map/all_gather | solution.py:52
  332.1 8.3 %fusion.135 = f32[4,192,1536]{2,1,0:T(8,128)} fusion(bf16[4,192,768]{2,1,0:T(8,128)(2,1)} %bitcast.298, bf16[4,768,1536]{2,1,0:T(8,128)(2,1)} %bitcast.279), kind=kOutput, calls=%fused_computation.293 | convolution fusion | flops 1811939328 | bytes 15335424 | tf_op jit(solution)/shard_map/ecd,edf->ecf/dot_general | solution.py:296
  340.5 7.0 fusion.129
  359.8 9.8 %fusion.6 = bf16[4,192,1536]{2,1,0:T(8,128)(2,1)S(1)} fusion(f32[4,192,1536]{2,1,0:T(8,128)} %fusion.135, bf16[4,192,768]{2,1,0:T(8,128)(2,1)S(1)} %bitcast.321, bf16[4,768,1536]{2,1,0:T(8,128)(2,1)} %bitcast.293), kind=kOutput, calls=%fused_computation.10 | convolution fusion | flops 1835532288 | bytes 17694720 | tf_op jit(solution)/shard_map/ecd,edf->ecf/dot_general | solution.py:316
  369.6 9.2 %convolution_convert_fusion = bf16[4,768,1536]{2,1,0:T(8,128)(2,1)} fusion(bf16[4,192,768]{2,1,0:T(8,128)(2,1)} %bitcast.322, f32[4,192,1536]{2,1,0:T(8,128)} %fusion.135), kind=kOutput, calls=%fused_computation | convolution fusion | flops 1827274752 | bytes 15335424 | tf_op jit(solution)/shard_map/ecd,ecf->edf/dot_general | solution.py:314
  388.6 6.2 slice.112
  397.4 5.6 constant_dynamic-slice_fusion.1
  408.3 8.1 %copy.65 = bf16[4,16,48,1536]{3,2,0,1:T(8,128)(2,1)} copy(bf16[4,16,48,1536]{3,2,1,0:T(8,128)(2,1)} %bitcast.284) | data formatting | bytes 18874368 | tf_op jit(solution)/shard_map/reshape | solution.py:311
  424.2 8.1 %copy.67 = bf16[4,16,48,1536]{3,2,0,1:T(8,128)(2,1)} copy(bf16[4,16,48,1536]{3,2,1,0:T(8,128)(2,1)} %bitcast.286) | data formatting | bytes 18874368 | tf_op jit(solution)/shard_map/reshape | solution.py:311
  441.1 8.8 %shard_map.248 = (bf16[512,384]{1,0:T(8,128)(2,1)S(1)}, bf16[512,384]{1,0:T(8,128)(2,1)S(1)}, bf16[512,384]{1,0:T(8,128)(2,1)S(1)}, f32[3,2,512]{2,1,0:T(2,128)S(1)}) custom-call(bf16[512,384]{1,0:T(8,128)(2,1)S(1)} %convolution_convert_fusion.9.q_ref, bf16[512,384]{1,0:T(8,128)(2,1)S(1)} %convolution_convert_fusion.8.k_ref, ...), custom_call_target="tpu_custom_call" | custom-call | flops 2013265920 | bytes 3145728 | tf_op jit(solution)/shard_map/pallas_call | solution.py:171
  466.4 10.7 %collective-permute-done.10 = bf16[4,2,2,48,384]{4,3,2,1,0:T(8,128)(2,1)} collective-permute-done((bf16[4,2,2,48,384]{4,3,2,1,0:T(8,128)(2,1)}, bf16[4,2,2,48,384]{4,3,2,1,0:T(8,128)(2,1)}, u32[]{:S(2)}, u32[]{:S(2)}) %collective-permute-start.10) | collective-permute-done | bytes 589856 | tf_op jit(solution)/shard_map/ppermute | solution.py:66
  480.7 42.6 %collective-permute-done.8 = bf16[4,2,2,48,384]{4,3,2,0,1:T(8,128)(2,1)} collective-permute-done((bf16[4,2,2,48,384]{4,3,2,0,1:T(8,128)(2,1)}, bf16[4,2,2,48,384]{4,3,2,0,1:T(8,128)(2,1)}, u32[]{:S(2)}, u32[]{:S(2)}) %collective-permute-start.8) | collective-permute-done | bytes 589856 | tf_op jit(solution)/shard_map/ppermute | solution.py:66
  530.4 38.6 %psum.7 = f32[4992]{0:T(1024)S(1)} all-reduce(f32[4992]{0:T(1024)S(1)} %pad_maximum_fusion.6), channel_id=1, replica_groups=mesh['fsdp'=16,'tp'=2] {'fsdp','tp'}, use_global_device_ids=true, to_apply=%region_12.13 | all-reduce | flops 4992 | bytes 39936 | tf_op jit(solution)/shard_map/psum | solution.py:371
  595.5 37.5 %collective-permute-done.30 = bf16[4,2,2,48,1536]{4,3,2,1,0:T(8,128)(2,1)S(1)} collective-permute-done((bf16[4,2,2,48,1536]{4,3,2,1,0:T(8,128)(2,1)}, bf16[4,2,2,48,1536]{4,3,2,1,0:T(8,128)(2,1)S(1)}, u32[]{:S(2)}, u32[]{:S(2)}) %collective-permute-start.30) | collective-permute-done | bytes 2359328 | tf_op jit(solution)/shard_map/ppermute | solution.py:66
  635.8 22.5 %collective-permute-done.19 = bf16[4,2,48,1536]{3,2,1,0:T(8,128)(2,1)S(1)} collective-permute-done((bf16[4,2,48,1536]{3,2,1,0:T(8,128)(2,1)S(1)}, bf16[4,2,48,1536]{3,2,1,0:T(8,128)(2,1)S(1)}, u32[]{:S(2)}, u32[]{:S(2)}) %collective-permute-start.19) | collective-permute-done | bytes 1179680 | tf_op jit(solution)/shard_map/ppermute | solution.py:66
  665.4 15.8 %collective-permute-done.29 = bf16[4,2,48,1536]{3,2,1,0:T(8,128)(2,1)S(1)} collective-permute-done((bf16[4,2,48,1536]{3,2,1,0:T(8,128)(2,1)S(1)}, bf16[4,2,48,1536]{3,2,1,0:T(8,128)(2,1)S(1)}, u32[]{:S(2)}, u32[]{:S(2)}) %collective-permute-start.29) | collective-permute-done | bytes 1179680 | tf_op jit(solution)/shard_map/ppermute | solution.py:66
  707.3 8.9 %collective-permute-done.23 = bf16[4,48,1536]{2,1,0:T(8,128)(2,1)S(1)} collective-permute-done((bf16[4,48,1536]{2,1,0:T(8,128)(2,1)S(1)}, bf16[4,48,1536]{2,1,0:T(8,128)(2,1)S(1)}, u32[]{:S(2)}, u32[]{:S(2)}) %collective-permute-start.23) | collective-permute-done | bytes 589856 | tf_op jit(solution)/shard_map/ppermute | solution.py:85
  722.3 6.6 collective-permute-done.33
  742.7 7.6 collective-permute-done.34
  (302 shorter events, 182.5 us)
Async XLA Ops:
  7.2 69.2 %all-gather.7.cloned.1.call-start = ((), (), s32[]{:S(2)}) async-start(), calls=%async_computation | async-start | bytes 2506752 | tf_op jit(solution)/shard_map/all_gather | solution.py:52
  8.9 191.7 %all-gather.9.cloned.1.call-start = ((), (), s32[]{:S(2)}) async-start(), calls=%async_computation.1 | async-start | bytes 10027008 | tf_op jit(solution)/shard_map/all_gather | solution.py:52
  9.6 314.4 %all-gather.11.cloned.1.call-start = ((), (), s32[]{:S(2)}) async-start(), calls=%async_computation.2 | async-start | bytes 10027008 | tf_op jit(solution)/shard_map/all_gather | solution.py:52
  385.0 34.2 %collective-permute-start.5 = (f32[256,768]{1,0:T(8,128)}, f32[256,768]{1,0:T(8,128)}, u32[]{:S(2)}, u32[]{:S(2)}) collective-permute-start(f32[256,768]{1,0:T(8,128)} %constant_dynamic-slice_fusion.8), channel_id=1, source_target_pairs={{0,1},{1,0},{2,3},{3,2},{4,5},{5,4},{6,7},{7,6},{8,9},{9,8},{10,11... | collective-permute-start | bytes 2359304 | tf_op jit(solution)/shard_map/ppermute | solution.py:32
  406.2 178.8 %collective-permute-start.18 = (bf16[4,2,2,48,1536]{4,3,2,0,1:T(8,128)(2,1)}, bf16[4,2,2,48,1536]{4,3,2,0,1:T(8,128)(2,1)}, u32[]{:S(2)}, u32[]{:S(2)}) collective-permute-start(bf16[4,2,2,48,1536]{4,3,2,0,1:T(8,128)(2,1)} %bitcast.274), channel_id=1, source_target_pairs={{0,2},{2,0},{4,6},{6,4},{8,10},{10,8},{12,14},{14,12},{16,18},{18,... | collective-permute-start | bytes 7077896 | tf_op jit(solution)/shard_map/ppermute | solution.py:66
  407.7 180.6 %collective-permute-start.28 = (bf16[4,2,2,48,1536]{4,3,2,0,1:T(8,128)(2,1)}, bf16[4,2,2,48,1536]{4,3,2,0,1:T(8,128)(2,1)}, u32[]{:S(2)}, u32[]{:S(2)}) collective-permute-start(bf16[4,2,2,48,1536]{4,3,2,0,1:T(8,128)(2,1)} %bitcast.273), channel_id=1, source_target_pairs={{0,2},{2,0},{4,6},{6,4},{8,10},{10,8},{12,14},{14,12},{16,18},{18,... | collective-permute-start | bytes 7077896 | tf_op jit(solution)/shard_map/ppermute | solution.py:66
  462.5 60.7 %collective-permute-start.8 = (bf16[4,2,2,48,384]{4,3,2,0,1:T(8,128)(2,1)}, bf16[4,2,2,48,384]{4,3,2,0,1:T(8,128)(2,1)}, u32[]{:S(2)}, u32[]{:S(2)}) collective-permute-start(bf16[4,2,2,48,384]{4,3,2,0,1:T(8,128)(2,1)} %bitcast.275), channel_id=1, source_target_pairs={{0,2},{2,0},{4,6},{6,4},{8,10},{10,8},{12,14},{14,12},{16,18},{18,... | collective-permute-start | bytes 1769480 | tf_op jit(solution)/shard_map/ppermute | solution.py:66
  465.9 61.0 %collective-permute-start.7 = (f32[256,768]{1,0:T(8,128)}, f32[256,768]{1,0:T(8,128)}, u32[]{:S(2)}, u32[]{:S(2)}) collective-permute-start(f32[256,768]{1,0:T(8,128)} %constant_dynamic-slice_fusion.7), channel_id=1, source_target_pairs={{0,1},{1,0},{2,3},{3,2},{4,5},{5,4},{6,7},{7,6},{8,9},{9,8},{10,11... | collective-permute-start | bytes 2359304 | tf_op jit(solution)/shard_map/ppermute | solution.py:32
  477.1 114.0 %collective-permute-start.20 = (bf16[4,2,2,48,1536]{4,3,2,1,0:T(8,128)(2,1)}, bf16[4,2,2,48,1536]{4,3,2,1,0:T(8,128)(2,1)}, u32[]{:S(2)}, u32[]{:S(2)}) collective-permute-start(bf16[4,2,2,48,1536]{4,3,2,1,0:T(8,128)(2,1)} %dynamic-slice_bitcast_fusion.1), channel_id=1, source_target_pairs={{0,4},{2,6},{4,0},{6,2},{8,12},{10,14},{12,8},{14,10},{16,20},{18,... | collective-permute-start | bytes 7077896 | tf_op jit(solution)/shard_map/ppermute | solution.py:66
  523.3 45.8 %collective-permute-start.11 = (bf16[4,2,48,384]{3,2,1,0:T(8,128)(2,1)}, bf16[4,2,48,384]{3,2,1,0:T(8,128)(2,1)}, u32[]{:S(2)}, u32[]{:S(2)}) collective-permute-start(bf16[4,2,48,384]{3,2,1,0:T(8,128)(2,1)} %dynamic-slice_bitcast_fusion.7), channel_id=1, source_target_pairs={{0,2},{2,0},{4,6},{6,4},{8,10},{10,8},{12,14},{14,12},{16,18},{18,... | collective-permute-start | bytes 884744 | tf_op jit(solution)/shard_map/ppermute | solution.py:66
  526.9 43.3 %collective-permute-start.9 = (bf16[4,2,48,384]{3,2,1,0:T(8,128)(2,1)}, bf16[4,2,48,384]{3,2,1,0:T(8,128)(2,1)}, u32[]{:S(2)}, u32[]{:S(2)}) collective-permute-start(bf16[4,2,48,384]{3,2,1,0:T(8,128)(2,1)} %dynamic-slice_bitcast_fusion.8), channel_id=1, source_target_pairs={{0,4},{2,6},{4,0},{6,2},{8,12},{10,14},{12,8},{14,10},{16,20},{18,... | collective-permute-start | bytes 884744 | tf_op jit(solution)/shard_map/ppermute | solution.py:66
  578.3 54.7 %collective-permute-start.30 = (bf16[4,2,2,48,1536]{4,3,2,1,0:T(8,128)(2,1)}, bf16[4,2,2,48,1536]{4,3,2,1,0:T(8,128)(2,1)S(1)}, u32[]{:S(2)}, u32[]{:S(2)}) collective-permute-start(bf16[4,2,2,48,1536]{4,3,2,1,0:T(8,128)(2,1)} %dynamic-slice_bitcast_fusion), channel_id=1, source_target_pairs={{0,4},{2,6},{4,0},{6,2},{8,12},{10,14},{12,8},{14,10},{16,20},{18,... | collective-permute-start | bytes 7077896 | tf_op jit(solution)/shard_map/ppermute | solution.py:66
  580.7 106.0 %collective-permute-start.13 = (bf16[4,48,384]{2,1,0:T(8,128)(2,1)S(1)}, bf16[4,48,384]{2,1,0:T(8,128)(2,1)S(1)}, u32[]{:S(2)}, u32[]{:S(2)}) collective-permute-start(bf16[4,48,384]{2,1,0:T(8,128)(2,1)S(1)} %get-tuple-element.67), channel_id=1, source_target_pairs={{0,8},{2,10},{4,12},{6,14},{8,16},{10,18},{12,20},{14,22},{1,9},{3... | collective-permute-start | bytes 442376 | tf_op jit(solution)/shard_map/ppermute | solution.py:85
  585.0 102.4 %collective-permute-start.16 = (bf16[4,48,384]{2,1,0:T(8,128)(2,1)S(1)}, bf16[4,48,384]{2,1,0:T(8,128)(2,1)S(1)}, u32[]{:S(2)}, u32[]{:S(2)}) collective-permute-start(bf16[4,48,384]{2,1,0:T(8,128)(2,1)S(1)} %get-tuple-element.68), channel_id=1, source_target_pairs={{16,8},{18,10},{20,12},{22,14},{24,16},{26,18},{28,20},{30,22},{17... | collective-permute-start | bytes 442376 | tf_op jit(solution)/shard_map/ppermute | solution.py:88
  588.3 69.9 %collective-permute-start.19 = (bf16[4,2,48,1536]{3,2,1,0:T(8,128)(2,1)S(1)}, bf16[4,2,48,1536]{3,2,1,0:T(8,128)(2,1)S(1)}, u32[]{:S(2)}, u32[]{:S(2)}) collective-permute-start(bf16[4,2,48,1536]{3,2,1,0:T(8,128)(2,1)S(1)} %dynamic-slice_bitcast_fusion.5), channel_id=1, source_target_pairs={{0,4},{2,6},{4,0},{6,2},{8,12},{10,14},{12,8},{14,10},{16,20},{18,... | collective-permute-start | bytes 3538952 | tf_op jit(solution)/shard_map/ppermute | solution.py:66
  591.1 90.1 %collective-permute-start.29 = (bf16[4,2,48,1536]{3,2,1,0:T(8,128)(2,1)S(1)}, bf16[4,2,48,1536]{3,2,1,0:T(8,128)(2,1)S(1)}, u32[]{:S(2)}, u32[]{:S(2)}) collective-permute-start(bf16[4,2,48,1536]{3,2,1,0:T(8,128)(2,1)S(1)} %dynamic-slice_bitcast_fusion.3), channel_id=1, source_target_pairs={{0,4},{2,6},{4,0},{6,2},{8,12},{10,14},{12,8},{14,10},{16,20},{18,... | collective-permute-start | bytes 3538952 | tf_op jit(solution)/shard_map/ppermute | solution.py:66
  633.0 27.6 %collective-permute-start.21 = (bf16[4,2,48,1536]{3,2,1,0:T(8,128)(2,1)S(1)}, bf16[4,2,48,1536]{3,2,1,0:T(8,128)(2,1)S(1)}, u32[]{:S(2)}, u32[]{:S(2)}) collective-permute-start(bf16[4,2,48,1536]{3,2,1,0:T(8,128)(2,1)S(1)} %dynamic-slice_bitcast_fusion.4), channel_id=1, source_target_pairs={{0,2},{2,0},{4,6},{6,4},{8,10},{10,8},{12,14},{14,12},{16,18},{18,... | collective-permute-start | bytes 3538952 | tf_op jit(solution)/shard_map/ppermute | solution.py:66
  658.3 24.1 %collective-permute-start.31 = (bf16[4,2,48,1536]{3,2,1,0:T(8,128)(2,1)S(1)}, bf16[4,2,48,1536]{3,2,1,0:T(8,128)(2,1)S(1)}, u32[]{:S(2)}, u32[]{:S(2)}) collective-permute-start(bf16[4,2,48,1536]{3,2,1,0:T(8,128)(2,1)S(1)} %dynamic-slice_bitcast_fusion.2), channel_id=1, source_target_pairs={{0,2},{2,0},{4,6},{6,4},{8,10},{10,8},{12,14},{14,12},{16,18},{18,... | collective-permute-start | bytes 3538952 | tf_op jit(solution)/shard_map/ppermute | solution.py:66
  661.1 27.7 %collective-permute-start.22 = (bf16[4,48,1536]{2,1,0:T(8,128)(2,1)S(1)}, bf16[4,48,1536]{2,1,0:T(8,128)(2,1)S(1)}, u32[]{:S(2)}, u32[]{:S(2)}) collective-permute-start(bf16[4,48,1536]{2,1,0:T(8,128)(2,1)S(1)} %get-tuple-element.45), channel_id=1, source_target_pairs={{0,8},{2,10},{4,12},{6,14},{1,9},{3,11},{5,13},{7,15}} | collective-permute-start | bytes 1769480 | tf_op jit(solution)/shard_map/ppermute | solution.py:85
  690.5 25.7 %collective-permute-start.23 = (bf16[4,48,1536]{2,1,0:T(8,128)(2,1)S(1)}, bf16[4,48,1536]{2,1,0:T(8,128)(2,1)S(1)}, u32[]{:S(2)}, u32[]{:S(2)}) collective-permute-start(bf16[4,48,1536]{2,1,0:T(8,128)(2,1)S(1)} %get-tuple-element.43), channel_id=1, source_target_pairs={{0,8},{2,10},{4,12},{6,14},{8,16},{10,18},{12,20},{14,22},{1,9},{3... | collective-permute-start | bytes 1769480 | tf_op jit(solution)/shard_map/ppermute | solution.py:85
  701.5 27.4 %collective-permute-start.33 = (bf16[4,48,1536]{2,1,0:T(8,128)(2,1)S(1)}, bf16[4,48,1536]{2,1,0:T(8,128)(2,1)S(1)}, u32[]{:S(2)}, u32[]{:S(2)}) collective-permute-start(bf16[4,48,1536]{2,1,0:T(8,128)(2,1)S(1)} %get-tuple-element.37), channel_id=1, source_target_pairs={{0,8},{2,10},{4,12},{6,14},{8,16},{10,18},{12,20},{14,22},{1,9},{3... | collective-permute-start | bytes 1769480 | tf_op jit(solution)/shard_map/ppermute | solution.py:85
  706.5 22.4 %collective-permute-start.36 = (bf16[4,48,1536]{2,1,0:T(8,128)(2,1)S(1)}, bf16[4,48,1536]{2,1,0:T(8,128)(2,1)S(1)}, u32[]{:S(2)}, u32[]{:S(2)}) collective-permute-start(bf16[4,48,1536]{2,1,0:T(8,128)(2,1)S(1)} %get-tuple-element.38), channel_id=1, source_target_pairs={{16,8},{18,10},{20,12},{22,14},{24,16},{26,18},{28,20},{30,22},{17... | collective-permute-start | bytes 1769480 | tf_op jit(solution)/shard_map/ppermute | solution.py:88
  716.5 24.9 %collective-permute-start.24 = (bf16[4,48,1536]{2,1,0:T(8,128)(2,1)S(1)}, bf16[4,48,1536]{2,1,0:T(8,128)(2,1)S(1)}, u32[]{:S(2)}, u32[]{:S(2)}) collective-permute-start(bf16[4,48,1536]{2,1,0:T(8,128)(2,1)S(1)} %get-tuple-element.41), channel_id=1, source_target_pairs={{0,8},{2,10},{4,12},{6,14},{8,16},{10,18},{12,20},{14,22},{16,24},... | collective-permute-start | bytes 1769480 | tf_op jit(solution)/shard_map/ppermute | solution.py:85
  729.2 21.1 %collective-permute-start.34 = (bf16[4,48,1536]{2,1,0:T(8,128)(2,1)S(1)}, bf16[4,48,1536]{2,1,0:T(8,128)(2,1)S(1)}, u32[]{:S(2)}, u32[]{:S(2)}) collective-permute-start(bf16[4,48,1536]{2,1,0:T(8,128)(2,1)S(1)} %get-tuple-element.35), channel_id=1, source_target_pairs={{0,8},{2,10},{4,12},{6,14},{8,16},{10,18},{12,20},{14,22},{16,24},... | collective-permute-start | bytes 1769480 | tf_op jit(solution)/shard_map/ppermute | solution.py:85
  (71 other events, 1187.1 us)
Sparse Core Ops, SparseCore 0:
  11.5 64.9 all-gather.6
  79.3 121.2 all-gather.8
  203.4 120.6 all-gather.10

commit v2 on v1

--- a/solution.py
+++ b/solution.py
@@ -48,57 +48,104 @@
     return keep + tp_swap(away)
 
 
-def fsdp_gather(shard):
-    return lax.all_gather(shard, "fsdp", axis=0, tiled=False)
+def grid_place():
+    index = lax.axis_index("fsdp")
+    return index // 4, (index // 2) % 2, index % 2
+
+
+def flip(values, bit):
+    return lax.ppermute(values, "fsdp", [(i, i ^ bit) for i in range(16)])
+
+
+def z_shift(values, step):
+    return lax.ppermute(values, "fsdp", [(i, (i + 4 * step) % 16) for i in range(16)])
 
 
 def add_low(left, right):
     return (left.astype(F32) + right.astype(F32)).astype(BF16)
 
 
-def scatter_grid(blocks):
-    index = lax.axis_index("fsdp")
-    z_at, y_at, x_at = index // 4, (index // 2) % 2, index % 2
-    grid = blocks.reshape((4, 2, 2) + blocks.shape[1:])
-    half = blocks.shape[1] // 2
-
-    def flip(values, bit):
-        return lax.ppermute(values, "fsdp", [(i, i ^ bit) for i in range(16)])
-
-    def fold(part, place, axis, bit):
-        away = lax.dynamic_index_in_dim(part, 1 - place, axis, False)
-        keep = lax.dynamic_index_in_dim(part, place, axis, False)
-        return add_low(keep, flip(away, bit))
-
-    first = fold(fold(grid[:, :, :, :half], x_at, 2, 1), y_at, 1, 2)
-    second = fold(fold(grid[:, :, :, half:], y_at, 1, 2), x_at, 1, 1)
-    column = jnp.concatenate([first, second], axis=1)
-
-    def pick(target):
-        return lax.dynamic_index_in_dim(column, jnp.clip(target, 0, 3), 0, False)
-
-    rising = falling = None
-    for offset in (3, 2, 1):
-        up, down = pick(z_at + offset), pick(z_at - offset)
-        if rising is not None:
-            up, down = add_low(up, rising), add_low(down, falling)
-        rising = lax.ppermute(
-            up, "fsdp", [(i, i + 4) for i in range(12) if i // 4 + offset <= 3]
-        )
-        falling = lax.ppermute(
-            down, "fsdp", [(i, i - 4) for i in range(4, 16) if i // 4 - offset >= 0]
-        )
-    return pick(z_at).astype(F32) + rising.astype(F32) + falling.astype(F32)
-
-
-def fsdp_scatter(blocks):
-    if USE_GRID and blocks.shape[0] == 16:
-        return scatter_grid(blocks.astype(BF16))
-    low = blocks.astype(BF16)
-    flat = low.reshape((-1, low.shape[-1]))
-    return lax.psum_scatter(flat, "fsdp", scatter_dimension=0, tiled=True).astype(F32).reshape(
-        blocks.shape[1:]
-    )
+def fsdp_gather(shard):
+    count = shard.shape[0] // 2
+    if lax.axis_size("fsdp") != 16:
+        full = lax.all_gather(shard, "fsdp", axis=1, tiled=True)
+        return full[:count], full[count:]
+    z_at, y_at, x_at = grid_place()
+    one, two, three = (z_shift(shard, step) for step in (1, 2, 3))
+    line = [three, two, one, shard, three, two, one]
+
+    def column(part):
+        stacked = jnp.stack([item[part] for item in line], axis=1)
+        return lax.dynamic_slice_in_dim(stacked, 3 - z_at, 4, 1)
+
+    def spread(part, place, axis, bit):
+        other = flip(part, bit)
+        low = jnp.where(place == 0, part, other)
+        high = jnp.where(place == 0, other, part)
+        return jnp.stack([low, high], axis=axis)
+
+    first = spread(spread(column(slice(0, count)), x_at, 2, 1), y_at, 2, 2)
+    second = spread(spread(column(slice(count, None)), y_at, 2, 2), x_at, 3, 1)
+    return tuple(
+        part.reshape(count, 16 * shard.shape[1], shard.shape[2]) for part in (first, second)
+    )
+
+
+def fold_parts(part, place, axis):
+    away = lax.dynamic_index_in_dim(part, 1 - place, axis, False)
+    keep = lax.dynamic_index_in_dim(part, place, axis, False)
+    return away, keep
+
+
+def scatter_first(halves):
+    _, y_at, x_at = grid_place()
+    first, second = (
+        half.reshape((half.shape[0], 4, 2, 2, half.shape[1] // 16, half.shape[2]))
+        for half in halves
+    )
+    return fold_parts(first, x_at, 3) + fold_parts(second, y_at, 2)
+
+
+def scatter_second(parts):
+    _, y_at, x_at = grid_place()
+    away_one, keep_one, away_two, keep_two = parts
+    first = add_low(keep_one, flip(away_one, 1))
+    second = add_low(keep_two, flip(away_two, 2))
+    return fold_parts(first, y_at, 2) + fold_parts(second, x_at, 2)
+
+
+def scatter_third(parts):
+    z_at, _, _ = grid_place()
+    away_one, keep_one, away_two, keep_two = parts
+    first = add_low(keep_one, flip(away_one, 2))
+    second = add_low(keep_two, flip(away_two, 1))
+    column = jnp.concatenate([first, second], axis=0)
+
+    def pick(step):
+        return lax.dynamic_index_in_dim(column, (z_at + step) % 4, 1, False)
+
+    total = pick(0).astype(F32)
+    for step in (1, 2, 3):
+        total = total + z_shift(pick(step), step).astype(F32)
+    return total
+
+
+def plain_scatter(halves):
+    full = jnp.concatenate(halves, axis=0)
+    return lax.psum_scatter(full, "fsdp", scatter_dimension=1, tiled=True).astype(F32)
+
+
+def after(values, earlier):
+    return lax.optimization_barrier((values, earlier))
+
+
+def sum_all(values):
+    if lax.axis_size("fsdp") != 16:
+        return lax.psum(values, ("fsdp", "tp"))
+    values = values + tp_swap(values)
+    for bit in (1, 2, 4, 8):
+        values = values + flip(values, bit)
+    return values
 
 
 def head_weights(query, key, window, same, rows):
@@ -210,9 +257,6 @@
     bucket_count, head_count = bias_table.shape
     expert_count = router.shape[1]
     slot_count = expert_count * CAP
-    hidden_width = w_in.shape[2]
-    head_width = w_query.shape[1]
-    shard_rows = w_query.shape[0]
     n_fsdp = lax.axis_size("fsdp")
     span_len = buckets.shape[0]
     max_len = (span_len + 1) // 2
@@ -221,16 +265,12 @@
     expert_ids = jnp.arange(expert_count, dtype=jnp.int32)
 
     attn_shard = jnp.stack([w_query, w_key, w_value, w_output.T])
-    attn_all = fsdp_gather(attn_shard)
-    inner_all = fsdp_gather(w_in)
-    outer_all = fsdp_gather(jnp.transpose(w_out, (0, 2, 1)))
-    attn_full = jnp.transpose(attn_all, (1, 0, 2, 3)).reshape(4, model_width, head_width)
-    inner_full = jnp.transpose(inner_all, (1, 0, 2, 3)).reshape(
-        expert_count, model_width, hidden_width
-    )
-    outer_full = jnp.transpose(outer_all, (1, 0, 2, 3)).reshape(
-        expert_count, model_width, hidden_width
-    )
+    attn_low, attn_high = fsdp_gather(attn_shard)
+    inner_halves = fsdp_gather(w_in)
+    outer_halves = fsdp_gather(jnp.transpose(w_out, (0, 2, 1)))
+    attn_full = (attn_low[0], attn_low[1], attn_high[0], attn_high[1])
+    on_grid = n_fsdp == 16
+    half_count = expert_count // 2
 
     inputs = tokens.astype(F32)
     gain_one = gain_attn.astype(F32)
@@ -292,34 +332,42 @@
             collect, low, preferred_element_type=F32
         )
 
-    buffer = to_slots(rows_two)
-    pre_act = jnp.einsum("ecd,edf->ecf", buffer, inner_full, preferred_element_type=F32)
-    activated = jax.nn.gelu(pre_act).astype(BF16)
-    expert_rows = jnp.einsum(
-        "ecf,edf->ecd", activated, outer_full, preferred_element_type=F32
-    ).reshape(slot_count, model_width)
+    def halves_of(values):
+        return values[:half_count], values[half_count:]
+
+    def rows_of(parts):
+        return jnp.concatenate(parts, axis=0).reshape(slot_count, model_width)
+
+    def product(spec, left, right):
+        return jnp.einsum(spec, left, right, preferred_element_type=F32)
+
+    buffers = halves_of(to_slots(rows_two))
+    pre_acts = [product("ecd,edf->ecf", b, w) for b, w in zip(buffers, inner_halves)]
+    activated = [jax.nn.gelu(pre).astype(BF16) for pre in pre_acts]
+    expert_rows = rows_of(
+        [product("ecf,edf->ecd", a, w) for a, w in zip(activated, outer_halves)]
+    )
     expert_val = tp_scatter(to_tokens(expert_rows))
     result = hidden + gate_val * expert_val
 
     grad_out = cotangent.astype(F32)
     grad_gate = jnp.sum(grad_out * expert_val, axis=-1, keepdims=True)
     grad_expert = (gate_val * grad_out).astype(BF16)
-    grad_slots = to_slots(tp_gather(grad_expert))
-
-    def blocked(grads, parts):
-        return jnp.transpose(
-            grads.astype(BF16).reshape(parts, n_fsdp, shard_rows, grads.shape[-1]), (1, 0, 2, 3)
-        )
-
-    grad_outer = jnp.einsum("ecd,ecf->edf", grad_slots, activated, preferred_element_type=F32)
-    outer_sum = fsdp_scatter(blocked(grad_outer, expert_count))
-    grad_act = jnp.einsum("ecd,edf->ecf", grad_slots, outer_full, preferred_element_type=F32)
-    grad_pre = jax.vjp(jax.nn.gelu, pre_act)[1](grad_act)[0].astype(BF16)
-    grad_inner = jnp.einsum("ecd,ecf->edf", buffer, grad_pre, preferred_element_type=F32)
-    inner_sum = fsdp_scatter(blocked(grad_inner, expert_count))
-    grad_buffer = jnp.einsum(
-        "ecf,edf->ecd", grad_pre, inner_full, preferred_element_type=F32
-    ).reshape(slot_count, model_width)
+    grad_slots = halves_of(to_slots(tp_gather(grad_expert)))
+    outer_grads = [
+        product("ecd,ecf->edf", g, a).astype(BF16) for g, a in zip(grad_slots, activated)
+    ]
+    grad_acts = [product("ecd,edf->ecf", g, w) for g, w in zip(grad_slots, outer_halves)]
+    grad_pres = [
+        jax.vjp(jax.nn.gelu, pre)[1](grad)[0].astype(BF16)
+        for pre, grad in zip(pre_acts, grad_acts)
+    ]
+    inner_grads = [
+        product("ecd,ecf->edf", b, g).astype(BF16) for b, g in zip(buffers, grad_pres)
+    ]
+    grad_buffer = rows_of(
+        [product("ecf,edf->ecd", g, w) for g, w in zip(grad_pres, inner_halves)]
+    )
     grad_logits = (grad_gate * gate_val * (own_hot - chances)).astype(BF16)
     grad_router = jnp.einsum("td,te->de", scaled_two, grad_logits, preferred_element_type=F32)
     grad_scaled_two = tp_scatter(to_tokens(grad_buffer)) + jnp.einsum(
@@ -329,6 +377,11 @@
     grad_hidden = grad_out + rms_back(grad_scaled_two * gain_two, normed_two, inverse_two)
     grad_attn = tp_gather(grad_hidden.astype(BF16))
     grad_mixed = jnp.dot(grad_attn, attn_full[3], preferred_element_type=F32).astype(BF16)
+    if on_grid:
+        outer_parts = scatter_second(scatter_first(outer_grads))
+        (inner_grads, grad_mixed), outer_parts = after((inner_grads, grad_mixed), outer_parts)
+        outer_sum = scatter_third(outer_parts)
+        inner_parts = scatter_second(scatter_first(inner_grads))
     grad_queries, grad_keys, grad_values, window_sums = attend_call(
         attend_back_kernel,
         3,
@@ -338,18 +391,23 @@
         seg_col,
         seg_row,
     )
-    attn_grads = jnp.stack(
-        [
-            lax.dot_general(left, right, TN, preferred_element_type=F32)
-            for left, right in (
-                (rows_one, grad_queries),
-                (rows_one, grad_keys),
-                (rows_one, grad_values),
-                (grad_attn, mixed_out),
-            )
-        ]
-    )
-    attn_sum = fsdp_scatter(blocked(attn_grads, 4))
+    attn_grads = [
+        jnp.stack(
+            [lax.dot_general(left, right, TN, preferred_element_type=F32) for left, right in pairs]
+        ).astype(BF16)
+        for pairs in (
+            ((rows_one, grad_queries), (rows_one, grad_keys)),
+            ((rows_one, grad_values), (grad_attn, mixed_out)),
+        )
+    ]
+    if on_grid:
+        attn_grads, inner_parts = after(attn_grads, inner_parts)
+        inner_sum = scatter_third(inner_parts)
+        attn_sum = scatter_third(scatter_second(scatter_first(attn_grads)))
+    else:
+        outer_sum, inner_sum, attn_sum = (
+            plain_scatter(grads) for grads in (outer_grads, inner_grads, attn_grads)
+        )
     grad_one_part = sum(
         lax.dot_general(grads, attn_full[i], NT, preferred_element_type=F32)
         for i, grads in enumerate((grad_queries, grad_keys, grad_values))
@@ -368,7 +426,7 @@
         0,
     )
     pieces = [grad_gain_one, grad_gain_two, grad_router.T.reshape(-1), table_full.reshape(-1)]
-    small = lax.psum(jnp.concatenate(pieces), ("fsdp", "tp"))
+    small = sum_all(jnp.concatenate(pieces))
     split = [0]
     for piece in pieces:
         split.append(split[-1] + piece.shape[0])
@@ -393,8 +451,6 @@
         jnp.transpose(outer_sum, (0, 2, 1)),
     )
 
-
-USE_GRID = True
 
 def solution(mesh):
     placed = (

time: 772 us -> 668 us (0.87)
  local copies, waits for them, and re-layouts: 76.8 us -> 33.1 us
  blocking collectives: 38.6 us -> 0 us
  starting transfers between devices: 61.7 us -> 84.3 us
  matrix products: 64.6 us -> 44.9 us
  waiting for transfers between devices: 451 us -> 432 us
  between operations: 15.3 us -> 2.67 us
  other arithmetic: 36.2 us -> 47.3 us
    all_gather x3 -> x0, waiting for transfers between devices: 277 us -> none  [fsdp_gather(): return lax.all_gather(shard, 'fsdp', axis=0, tiled=False)]
    ppermute x12 -> x28, waiting for transfers between devices: 129 us -> 282 us  [flip(): return lax.ppermute(values, 'fsdp', [(i, i ^ bit) for i in range(16)])]
    ppermute x18, waiting for transfers between devices: 36.3 us -> 148 us  [z_shift(): lax.ppermute(values, 'fsdp', [(i, (i + 4 * step) % 16) for i in range(16)])]
    psum x1 -> x0, blocking collectives: 38.6 us -> none  [on_device(): small = lax.psum(jnp.concatenate(pieces), ('fsdp', 'tp'))]
    ppermute x12 -> x28, starting transfers between devices: 15.9 us -> 35.4 us  [flip(): return lax.ppermute(values, 'fsdp', [(i, i ^ bit) for i in range(16)])]
    another operation x1 -> x25, other arithmetic: 0.18 us -> 17 us  [the longest x24 16.2 us: spread(): return jnp.stack([low, high], axis=axis)]
    reshape x3 -> x0, local copies, waits for them, and re-layouts: 16.3 us -> none  [the longest x2 16.2 us: blocked(): grads.astype(BF16).reshape(parts, n_fsdp, shard_rows, grads.shape[-1])]
    all_gather x2 -> x0, local copies, waits for them, and re-layouts: 16.2 us -> none  [fsdp_gather(): return lax.all_gather(shard, 'fsdp', axis=0, tiled=False)]
  transfers between devices with their start and end apart: 41 -> 55, of which waited for: 20 -> 26; matrix products, arithmetic and copies ran while one was open for 15% -> 13% of each run, Pallas kernels for 2% -> 1%
where the time goes in v2:
time: 668 us; the launch traced here: 661 us
  waiting for transfers between devices  432 us (65%)
  starting transfers between devices  84.3 us (13%)
  other arithmetic  47.3 us (7%)
  matrix products  44.9 us (7%)
  local copies, waits for them, and re-layouts  33.1 us (5%)
  Pallas kernels  16.5 us (2%)
    ppermute x28, waiting for transfers between devices, flip(): return lax.ppermute(values, 'fsdp', [(i, i ^ bit) for i in range(16)])  282 us
    ppermute x18, waiting for transfers between devices, z_shift(): lax.ppermute(values, 'fsdp', [(i, (i + 4 * step) % 16) for i in range(16)])  148 us
    ppermute x18, starting transfers between devices, z_shift(): lax.ppermute(values, 'fsdp', [(i, (i + 4 * step) % 16) for i in range(16)])  47.9 us
    ppermute x28, starting transfers between devices, flip(): return lax.ppermute(values, 'fsdp', [(i, i ^ bit) for i in range(16)])  35.4 us
    dot_general x12, matrix products, product(): return jnp.einsum(spec, left, right, preferred_element_type=F32)  26.6 us
    pallas_call x2, Pallas kernels, attend_call(): pl.pallas_call(kernel, grid=(steps,), in_specs=[wide] * len(wide_in) + [l...  16.5 us
    another operation x24, other arithmetic, spread(): return jnp.stack([low, high], axis=axis)  16.2 us
  transfers between devices with their start and end apart: 55, of which 26 were waited for; matrix products, arithmetic and copies ran while one was open for 13% of the time, Pallas kernels for 1%

profile of v2, /device:TPU:0, one launch (start us, length us, event | category | flops | bytes accessed | tf_op | source)
XLA Modules:
  0.0 661.3 jit_solution(3643056848511027196)
XLA Ops:
  0.7 5.1 collective-permute-start.15
  20.3 28.1 %collective-permute-done.1 = bf16[4,48,384]{2,1,0:T(8,128)(2,1)S(1)} collective-permute-done((bf16[4,48,384]{2,1,0:T(8,128)(2,1)}, bf16[4,48,384]{2,1,0:T(8,128)(2,1)S(1)}, u32[]{:S(2)}, u32[]{:S(2)}) %collective-permute-start.1) | collective-permute-done | bytes 147488 | tf_op jit(solution)/shard_map/ppermute | solution.py:61
  48.4 19.2 %collective-permute-start.3 = (bf16[4,48,384]{2,1,0:T(8,128)(2,1)}, bf16[4,48,384]{2,1,0:T(8,128)(2,1)S(1)}, u32[]{:S(2)}, u32[]{:S(2)}) collective-permute-start(bf16[4,48,384]{2,1,0:T(8,128)(2,1)} %pad_maximum_fusion.20), channel_id=1, source_target_pairs={{0,8},{2,10},{4,12},{6,14},{8,16},{10,18},{12,20},{14,22},{16,24},... | collective-permute-start | bytes 442376 | tf_op jit(solution)/shard_map/ppermute | solution.py:61
  74.9 3.8 collective-permute-done.4
  80.4 5.3 collective-permute-done.6
  94.4 29.9 %collective-permute-done.11 = bf16[4,48,1536]{2,1,0:T(8,128)(2,1)S(1)} collective-permute-done((bf16[4,48,1536]{2,1,0:T(8,128)(2,1)S(1)}, bf16[4,48,1536]{2,1,0:T(8,128)(2,1)S(1)}, u32[]{:S(2)}, u32[]{:S(2)}) %collective-permute-start.11) | collective-permute-done | bytes 589856 | tf_op jit(solution)/shard_map/ppermute | solution.py:61
  134.4 7.9 %shard_map.247 = bf16[512,384]{1,0:T(8,128)(2,1)S(1)} custom-call(bf16[512,384]{1,0:T(8,128)(2,1)S(1)} %convolution_convert_fusion.11.q_ref, bf16[512,384]{1,0:T(8,128)(2,1)S(1)} %convolution_convert_fusion.10.k_ref, bf16[512,384]{1,0:T(8,128)(2,1)S(1)} %convolution_convert_fusion.9.v_ref, f32[3,2,512]{2,1,0:T(2,128)S(1)} %reshape.185.win_ref, ...), custom_call_target="tpu_custom_call" | custom-call | flops 805306368 | bytes 3145728 | tf_op jit(solution)/shard_map/pallas_call | solution.py:218
  145.1 7.8 %collective-permute-done.20 = bf16[2,4,48,1536]{3,2,0,1:T(8,128)(2,1)} collective-permute-done((bf16[2,4,48,1536]{3,2,0,1:T(8,128)(2,1)}, bf16[2,4,48,1536]{3,2,0,1:T(8,128)(2,1)}, u32[]{:S(2)}, u32[]{:S(2)}) %collective-permute-start.20) | collective-permute-done | bytes 1179680 | tf_op jit(solution)/shard_map/ppermute | solution.py:57
  159.3 23.7 %collective-permute-done.13 = bf16[2,4,48,1536]{3,2,0,1:T(8,128)(2,1)} collective-permute-done((bf16[2,4,48,1536]{3,2,0,1:T(8,128)(2,1)}, bf16[2,4,48,1536]{3,2,0,1:T(8,128)(2,1)}, u32[]{:S(2)}, u32[]{:S(2)}) %collective-permute-start.13) | collective-permute-done | bytes 1179680 | tf_op jit(solution)/shard_map/ppermute | solution.py:57
  187.8 45.7 %collective-permute-done.23 = bf16[2,4,2,48,1536]{4,3,0,1,2:T(8,128)(2,1)} collective-permute-done((bf16[2,4,2,48,1536]{4,3,0,1,2:T(8,128)(2,1)S(1)}, bf16[2,4,2,48,1536]{4,3,0,1,2:T(8,128)(2,1)}, u32[]{:S(2)}, u32[]{:S(2)}) %collective-permute-start.23) | collective-permute-done | bytes 2359328 | tf_op jit(solution)/shard_map/ppermute | solution.py:57
  236.4 45.5 %collective-permute-done.21 = bf16[2,4,2,48,1536]{4,3,0,1,2:T(8,128)(2,1)S(1)} collective-permute-done((bf16[2,4,2,48,1536]{4,3,0,1,2:T(8,128)(2,1)S(1)}, bf16[2,4,2,48,1536]{4,3,0,1,2:T(8,128)(2,1)S(1)}, u32[]{:S(2)}, u32[]{:S(2)}) %collective-permute-start.21) | collective-permute-done | bytes 2359328 | tf_op jit(solution)/shard_map/ppermute | solution.py:57
  283.1 3.7 select_bitcast_fusion.5
  310.1 4.8 fusion.10
  331.4 3.7 convolution_convert_fusion.3
  340.8 38.3 %collective-permute-done.28 = bf16[2,4,2,48,1536]{4,3,2,1,0:T(8,128)(2,1)S(1)} collective-permute-done((bf16[2,4,2,48,1536]{4,3,2,1,0:T(8,128)(2,1)S(1)}, bf16[2,4,2,48,1536]{4,3,2,1,0:T(8,128)(2,1)S(1)}, u32[]{:S(2)}, u32[]{:S(2)}) %collective-permute-start.28) | collective-permute-done | bytes 2359328 | tf_op jit(solution)/shard_map/ppermute | solution.py:57
  386.6 8.6 %shard_map.248 = (bf16[512,384]{1,0:T(8,128)(2,1)S(1)}, bf16[512,384]{1,0:T(8,128)(2,1)S(1)}, bf16[512,384]{1,0:T(8,128)(2,1)S(1)}, f32[3,2,512]{2,1,0:T(2,128)S(1)}) custom-call(bf16[512,384]{1,0:T(8,128)(2,1)S(1)} %convolution_convert_fusion.11.q_ref, bf16[512,384]{1,0:T(8,128)(2,1)S(1)} %convolution_convert_fusion.10.k_ref, ...), custom_call_target="tpu_custom_call" | custom-call | flops 2013265920 | bytes 3145728 | tf_op jit(solution)/shard_map/pallas_call | solution.py:218
  417.7 64.7 %collective-permute-done.32 = f32[4992]{0:T(1024)S(1)} collective-permute-done((f32[4992]{0:T(1024)S(1)}, f32[4992]{0:T(1024)S(1)}, u32[]{:S(2)}, u32[]{:S(2)}) %collective-permute-start.32) | collective-permute-done | bytes 20000 | tf_op jit(solution)/shard_map/ppermute | solution.py:57
  484.0 7.7 %collective-permute-done.33 = f32[4992]{0:T(1024)S(1)} collective-permute-done((f32[4992]{0:T(1024)S(1)}, f32[4992]{0:T(1024)S(1)}, u32[]{:S(2)}, u32[]{:S(2)}) %collective-permute-start.33) | collective-permute-done | bytes 20000 | tf_op jit(solution)/shard_map/ppermute | solution.py:57
  496.0 3.9 collective-permute-start.35
  519.7 10.3 %collective-permute-done.38 = bf16[2,4,2,48,384]{4,3,0,1,2:T(8,128)(2,1)S(1)} collective-permute-done((bf16[2,4,2,48,384]{4,3,0,1,2:T(8,128)(2,1)S(1)}, bf16[2,4,2,48,384]{4,3,0,1,2:T(8,128)(2,1)S(1)}, u32[]{:S(2)}, u32[]{:S(2)}) %collective-permute-start.38) | collective-permute-done | bytes 589856 | tf_op jit(solution)/shard_map/ppermute | solution.py:57
  535.1 23.8 %collective-permute-done.39 = bf16[2,4,48,384]{3,2,0,1:T(8,128)(2,1)S(1)} collective-permute-done((bf16[2,4,48,384]{3,2,0,1:T(8,128)(2,1)S(1)}, bf16[2,4,48,384]{3,2,0,1:T(8,128)(2,1)S(1)}, u32[]{:S(2)}, u32[]{:S(2)}) %collective-permute-start.39) | collective-permute-done | bytes 294944 | tf_op jit(solution)/shard_map/ppermute | solution.py:57
  567.1 35.8 %collective-permute-done.53 = bf16[4,48,1536]{2,1,0:T(8,128)(2,1)S(1)} collective-permute-done((bf16[4,48,1536]{2,1,0:T(8,128)(2,1)S(1)}, bf16[4,48,1536]{2,1,0:T(8,128)(2,1)S(1)}, u32[]{:S(2)}, u32[]{:S(2)}) %collective-permute-start.53) | collective-permute-done | bytes 589856 | tf_op jit(solution)/shard_map/ppermute | solution.py:61
  610.1 11.1 %collective-permute-done.49 = bf16[4,48,1536]{2,1,0:T(8,128)(2,1)S(1)} collective-permute-done((bf16[4,48,1536]{2,1,0:T(8,128)(2,1)S(1)}, bf16[4,48,1536]{2,1,0:T(8,128)(2,1)S(1)}, u32[]{:S(2)}, u32[]{:S(2)}) %collective-permute-start.49) | collective-permute-done | bytes 589856 | tf_op jit(solution)/shard_map/ppermute | solution.py:61
  621.3 38.5 %collective-permute-done.48 = bf16[4,48,1536]{2,1,0:T(8,128)(2,1)S(1)} collective-permute-done((bf16[4,48,1536]{2,1,0:T(8,128)(2,1)S(1)}, bf16[4,48,1536]{2,1,0:T(8,128)(2,1)S(1)}, u32[]{:S(2)}, u32[]{:S(2)}) %collective-permute-start.48) | collective-permute-done | bytes 589856 | tf_op jit(solution)/shard_map/ppermute | solution.py:61
  (409 shorter events, 181.5 us)
Async XLA Ops:
  0.7 85.5 %collective-permute-start.15 = (bf16[4,48,1536]{2,1,0:T(8,128)(2,1)}, bf16[4,48,1536]{2,1,0:T(8,128)(2,1)S(1)}, u32[]{:S(2)}, u32[]{:S(2)}) collective-permute-start(bf16[4,48,1536]{2,1,0:T(8,128)(2,1)} %bitcast.446), channel_id=1, source_target_pairs={{0,24},{2,26},{4,28},{6,30},{8,0},{10,2},{12,4},{14,6},{16,8},{18,... | collective-permute-start | bytes 1769480 | tf_op jit(solution)/shard_map/ppermute | solution.py:61
  5.8 83.5 %collective-permute-start.16 = (bf16[4,48,1536]{2,1,0:T(8,128)(2,1)}, bf16[4,48,1536]{2,1,0:T(8,128)(2,1)S(1)}, u32[]{:S(2)}, u32[]{:S(2)}) collective-permute-start(bf16[4,48,1536]{2,1,0:T(8,128)(2,1)} %bitcast.447), channel_id=1, source_target_pairs={{0,16},{2,18},{4,20},{6,22},{8,24},{10,26},{12,28},{14,30},{16,0},... | collective-permute-start | bytes 1769480 | tf_op jit(solution)/shard_map/ppermute | solution.py:61
  5.8 85.1 %collective-permute-start.17 = (bf16[4,48,1536]{2,1,0:T(8,128)(2,1)}, bf16[4,48,1536]{2,1,0:T(8,128)(2,1)S(1)}, u32[]{:S(2)}, u32[]{:S(2)}) collective-permute-start(bf16[4,48,1536]{2,1,0:T(8,128)(2,1)} %bitcast.448), channel_id=1, source_target_pairs={{0,8},{2,10},{4,12},{6,14},{8,16},{10,18},{12,20},{14,22},{16,24},... | collective-permute-start | bytes 1769480 | tf_op jit(solution)/shard_map/ppermute | solution.py:61
  11.1 57.9 %collective-permute-start.2 = (bf16[4,48,384]{2,1,0:T(8,128)(2,1)}, bf16[4,48,384]{2,1,0:T(8,128)(2,1)S(1)}, u32[]{:S(2)}, u32[]{:S(2)}) collective-permute-start(bf16[4,48,384]{2,1,0:T(8,128)(2,1)} %pad_maximum_fusion.20), channel_id=1, source_target_pairs={{0,16},{2,18},{4,20},{6,22},{8,24},{10,26},{12,28},{14,30},{16,0},... | collective-permute-start | bytes 442376 | tf_op jit(solution)/shard_map/ppermute | solution.py:61
  93.9 49.2 %collective-permute-start.22 = (bf16[2,4,48,1536]{3,2,0,1:T(8,128)(2,1)}, bf16[2,4,48,1536]{3,2,0,1:T(8,128)(2,1)S(1)}, u32[]{:S(2)}, u32[]{:S(2)}) collective-permute-start(bf16[2,4,48,1536]{3,2,0,1:T(8,128)(2,1)} %constant_dynamic-slice_fusion.16), channel_id=1, source_target_pairs={{0,4},{2,6},{4,0},{6,2},{8,12},{10,14},{12,8},{14,10},{16,20},{18,... | collective-permute-start | bytes 3538952 | tf_op jit(solution)/shard_map/ppermute | solution.py:57
  131.1 51.9 %collective-permute-start.13 = (bf16[2,4,48,1536]{3,2,0,1:T(8,128)(2,1)}, bf16[2,4,48,1536]{3,2,0,1:T(8,128)(2,1)}, u32[]{:S(2)}, u32[]{:S(2)}) collective-permute-start(bf16[2,4,48,1536]{3,2,0,1:T(8,128)(2,1)} %constant_dynamic-slice_fusion.19), channel_id=1, source_target_pairs={{0,2},{2,0},{4,6},{6,4},{8,10},{10,8},{12,14},{14,12},{16,18},{18,... | collective-permute-start | bytes 3538952 | tf_op jit(solution)/shard_map/ppermute | solution.py:57
  143.5 90.0 %collective-permute-start.23 = (bf16[2,4,2,48,1536]{4,3,0,1,2:T(8,128)(2,1)S(1)}, bf16[2,4,2,48,1536]{4,3,0,1,2:T(8,128)(2,1)}, u32[]{:S(2)}, u32[]{:S(2)}) collective-permute-start(bf16[2,4,2,48,1536]{4,3,0,1,2:T(8,128)(2,1)S(1)} %pad_maximum_fusion.7), channel_id=1, source_target_pairs={{0,2},{2,0},{4,6},{6,4},{8,10},{10,8},{12,14},{14,12},{16,18},{18,... | collective-permute-start | bytes 7077896 | tf_op jit(solution)/shard_map/ppermute | solution.py:57
  154.7 127.2 %collective-permute-start.21 = (bf16[2,4,2,48,1536]{4,3,0,1,2:T(8,128)(2,1)S(1)}, bf16[2,4,2,48,1536]{4,3,0,1,2:T(8,128)(2,1)S(1)}, u32[]{:S(2)}, u32[]{:S(2)}) collective-permute-start(bf16[2,4,2,48,1536]{4,3,0,1,2:T(8,128)(2,1)S(1)} %pad_maximum_fusion.6), channel_id=1, source_target_pairs={{0,2},{2,0},{4,6},{6,4},{8,10},{10,8},{12,14},{14,12},{16,18},{18,... | collective-permute-start | bytes 7077896 | tf_op jit(solution)/shard_map/ppermute | solution.py:57
  158.0 125.1 %collective-permute-start.19 = (bf16[2,4,2,48,1536]{4,3,0,1,2:T(8,128)(2,1)S(1)}, bf16[2,4,2,48,1536]{4,3,0,1,2:T(8,128)(2,1)}, u32[]{:S(2)}, u32[]{:S(2)}) collective-permute-start(bf16[2,4,2,48,1536]{4,3,0,1,2:T(8,128)(2,1)S(1)} %pad_maximum_fusion.5), channel_id=1, source_target_pairs={{0,4},{2,6},{4,0},{6,2},{8,12},{10,14},{12,8},{14,10},{16,20},{18,... | collective-permute-start | bytes 7077896 | tf_op jit(solution)/shard_map/ppermute | solution.py:57
  186.1 103.5 %collective-permute-start.14 = (bf16[2,4,2,48,1536]{4,3,0,1,2:T(8,128)(2,1)}, bf16[2,4,2,48,1536]{4,3,0,1,2:T(8,128)(2,1)}, u32[]{:S(2)}, u32[]{:S(2)}) collective-permute-start(bf16[2,4,2,48,1536]{4,3,0,1,2:T(8,128)(2,1)} %pad_maximum_fusion.4), channel_id=1, source_target_pairs={{0,4},{2,6},{4,0},{6,2},{8,12},{10,14},{12,8},{14,10},{16,20},{18,... | collective-permute-start | bytes 7077896 | tf_op jit(solution)/shard_map/ppermute | solution.py:57
  325.5 53.6 %collective-permute-start.28 = (bf16[2,4,2,48,1536]{4,3,2,1,0:T(8,128)(2,1)S(1)}, bf16[2,4,2,48,1536]{4,3,2,1,0:T(8,128)(2,1)S(1)}, u32[]{:S(2)}, u32[]{:S(2)}) collective-permute-start(bf16[2,4,2,48,1536]{4,3,2,1,0:T(8,128)(2,1)S(1)} %dynamic-slice_bitcast_fusion.3), channel_id=1, source_target_pairs={{0,2},{2,0},{4,6},{6,4},{8,10},{10,8},{12,14},{14,12},{16,18},{18,... | collective-permute-start | bytes 7077896 | tf_op jit(solution)/shard_map/ppermute | solution.py:57
  329.1 53.3 %collective-permute-start.29 = (bf16[2,4,2,48,1536]{4,3,2,1,0:T(8,128)(2,1)S(1)}, bf16[2,4,2,48,1536]{4,3,2,1,0:T(8,128)(2,1)S(1)}, u32[]{:S(2)}, u32[]{:S(2)}) collective-permute-start(bf16[2,4,2,48,1536]{4,3,2,1,0:T(8,128)(2,1)S(1)} %dynamic-slice_bitcast_fusion.2), channel_id=1, source_target_pairs={{0,4},{2,6},{4,0},{6,2},{8,12},{10,14},{12,8},{14,10},{16,20},{18,... | collective-permute-start | bytes 7077896 | tf_op jit(solution)/shard_map/ppermute | solution.py:57
  402.8 102.4 %collective-permute-start.36 = (bf16[2,4,2,48,1536]{4,3,2,1,0:T(8,128)(2,1)}, bf16[2,4,2,48,1536]{4,3,2,1,0:T(8,128)(2,1)}, u32[]{:S(2)}, u32[]{:S(2)}) collective-permute-start(bf16[2,4,2,48,1536]{4,3,2,1,0:T(8,128)(2,1)} %dynamic-slice_bitcast_fusion.1), channel_id=1, source_target_pairs={{0,2},{2,0},{4,6},{6,4},{8,10},{10,8},{12,14},{14,12},{16,18},{18,... | collective-permute-start | bytes 7077896 | tf_op jit(solution)/shard_map/ppermute | solution.py:57
  412.3 96.6 %collective-permute-start.37 = (bf16[2,4,2,48,1536]{4,3,2,1,0:T(8,128)(2,1)}, bf16[2,4,2,48,1536]{4,3,2,1,0:T(8,128)(2,1)}, u32[]{:S(2)}, u32[]{:S(2)}) collective-permute-start(bf16[2,4,2,48,1536]{4,3,2,1,0:T(8,128)(2,1)} %dynamic-slice_bitcast_fusion), channel_id=1, source_target_pairs={{0,4},{2,6},{4,0},{6,2},{8,12},{10,14},{12,8},{14,10},{16,20},{18,... | collective-permute-start | bytes 7077896 | tf_op jit(solution)/shard_map/ppermute | solution.py:57
  412.9 90.7 %collective-permute-start.50 = (bf16[2,4,48,1536]{3,2,0,1:T(8,128)(2,1)}, bf16[2,4,48,1536]{3,2,0,1:T(8,128)(2,1)}, u32[]{:S(2)}, u32[]{:S(2)}) collective-permute-start(bf16[2,4,48,1536]{3,2,0,1:T(8,128)(2,1)} %get-tuple-element.43), channel_id=1, source_target_pairs={{0,4},{2,6},{4,0},{6,2},{8,12},{10,14},{12,8},{14,10},{16,20},{18,... | collective-permute-start | bytes 3538952 | tf_op jit(solution)/shard_map/ppermute | solution.py:57
  414.4 100.7 %collective-permute-start.51 = (bf16[2,4,48,1536]{3,2,0,1:T(8,128)(2,1)}, bf16[2,4,48,1536]{3,2,0,1:T(8,128)(2,1)}, u32[]{:S(2)}, u32[]{:S(2)}) collective-permute-start(bf16[2,4,48,1536]{3,2,0,1:T(8,128)(2,1)} %get-tuple-element.45), channel_id=1, source_target_pairs={{0,2},{2,0},{4,6},{6,4},{8,10},{10,8},{12,14},{14,12},{16,18},{18,... | collective-permute-start | bytes 3538952 | tf_op jit(solution)/shard_map/ppermute | solution.py:57
  416.2 66.2 %collective-permute-start.32 = (f32[4992]{0:T(1024)S(1)}, f32[4992]{0:T(1024)S(1)}, u32[]{:S(2)}, u32[]{:S(2)}) collective-permute-start(f32[4992]{0:T(1024)S(1)} %fusion.196), channel_id=1, source_target_pairs={{0,2},{2,0},{4,6},{6,4},{8,10},{10,8},{12,14},{14,12},{16,18},{18,... | collective-permute-start | bytes 59912 | tf_op jit(solution)/shard_map/ppermute | solution.py:57
  516.7 45.3 %collective-permute-start.45 = (bf16[2,4,48,1536]{3,2,0,1:T(8,128)(2,1)S(1)}, bf16[2,4,48,1536]{3,2,0,1:T(8,128)(2,1)S(1)}, u32[]{:S(2)}, u32[]{:S(2)}) collective-permute-start(bf16[2,4,48,1536]{3,2,0,1:T(8,128)(2,1)S(1)} %bitcast.444), channel_id=1, source_target_pairs={{0,4},{2,6},{4,0},{6,2},{8,12},{10,14},{12,8},{14,10},{16,20},{18,... | collective-permute-start | bytes 3538952 | tf_op jit(solution)/shard_map/ppermute | solution.py:57
  518.3 47.7 %collective-permute-start.46 = (bf16[2,4,48,1536]{3,2,0,1:T(8,128)(2,1)S(1)}, bf16[2,4,48,1536]{3,2,0,1:T(8,128)(2,1)S(1)}, u32[]{:S(2)}, u32[]{:S(2)}) collective-permute-start(bf16[2,4,48,1536]{3,2,0,1:T(8,128)(2,1)S(1)} %bitcast.445), channel_id=1, source_target_pairs={{0,2},{2,0},{4,6},{6,4},{8,10},{10,8},{12,14},{14,12},{16,18},{18,... | collective-permute-start | bytes 3538952 | tf_op jit(solution)/shard_map/ppermute | solution.py:57
  558.9 44.0 %collective-permute-start.53 = (bf16[4,48,1536]{2,1,0:T(8,128)(2,1)S(1)}, bf16[4,48,1536]{2,1,0:T(8,128)(2,1)S(1)}, u32[]{:S(2)}, u32[]{:S(2)}) collective-permute-start(bf16[4,48,1536]{2,1,0:T(8,128)(2,1)S(1)} %get-tuple-element.66), channel_id=1, source_target_pairs={{0,16},{2,18},{4,20},{6,22},{8,24},{10,26},{12,28},{14,30},{16,0},... | collective-permute-start | bytes 1769480 | tf_op jit(solution)/shard_map/ppermute | solution.py:61
  562.0 43.4 %collective-permute-start.44 = (bf16[4,48,384]{2,1,0:T(8,128)(2,1)S(1)}, bf16[4,48,384]{2,1,0:T(8,128)(2,1)S(1)}, u32[]{:S(2)}, u32[]{:S(2)}) collective-permute-start(bf16[4,48,384]{2,1,0:T(8,128)(2,1)S(1)} %get-tuple-element.115), channel_id=1, source_target_pairs={{0,24},{2,26},{4,28},{6,30},{8,0},{10,2},{12,4},{14,6},{16,8},{18,... | collective-permute-start | bytes 442376 | tf_op jit(solution)/shard_map/ppermute | solution.py:61
  565.9 43.4 %collective-permute-start.43 = (bf16[4,48,384]{2,1,0:T(8,128)(2,1)S(1)}, bf16[4,48,384]{2,1,0:T(8,128)(2,1)S(1)}, u32[]{:S(2)}, u32[]{:S(2)}) collective-permute-start(bf16[4,48,384]{2,1,0:T(8,128)(2,1)S(1)} %get-tuple-element.114), channel_id=1, source_target_pairs={{0,16},{2,18},{4,20},{6,22},{8,24},{10,26},{12,28},{14,30},{16,0},... | collective-permute-start | bytes 442376 | tf_op jit(solution)/shard_map/ppermute | solution.py:61
  602.9 56.8 %collective-permute-start.48 = (bf16[4,48,1536]{2,1,0:T(8,128)(2,1)S(1)}, bf16[4,48,1536]{2,1,0:T(8,128)(2,1)S(1)}, u32[]{:S(2)}, u32[]{:S(2)}) collective-permute-start(bf16[4,48,1536]{2,1,0:T(8,128)(2,1)S(1)} %get-tuple-element.69), channel_id=1, source_target_pairs={{0,16},{2,18},{4,20},{6,22},{8,24},{10,26},{12,28},{14,30},{16,0},... | collective-permute-start | bytes 1769480 | tf_op jit(solution)/shard_map/ppermute | solution.py:61
  605.4 54.4 %collective-permute-start.47 = (bf16[4,48,1536]{2,1,0:T(8,128)(2,1)S(1)}, bf16[4,48,1536]{2,1,0:T(8,128)(2,1)S(1)}, u32[]{:S(2)}, u32[]{:S(2)}) collective-permute-start(bf16[4,48,1536]{2,1,0:T(8,128)(2,1)S(1)} %get-tuple-element.68), channel_id=1, source_target_pairs={{0,8},{2,10},{4,12},{6,14},{8,16},{10,18},{12,20},{14,22},{16,24},... | collective-permute-start | bytes 1769480 | tf_op jit(solution)/shard_map/ppermute | solution.py:61
  (86 other events, 2102.4 us)
